TPU v7x, 256 devices: a whole 4x4x8 slice. The times are simulated.
256 devices in a mesh: layer: 8 (over y, z_lo), lat: 32 (over x, z_hi, core).
Axes of the slice: x: 4, y: 4, z: 8 (z_hi: 4, z_lo: 2; z = z_hi * 2 + z_lo), core: 2. Of those that a mesh axis runs over, the one named last changes fastest.
Arguments:
- acts: bfloat16 [8, 512, 2304], P('layer', 'lat'), may hold values from -6 to 6
- enc_weight: bfloat16 [8, 2304, 40960], P('layer', None, 'lat'), may hold values from -0.046875 to 0.046875
- enc_scale: float32 [8, 18, 320], P('layer', None, 'lat'), may hold values from 0.5 to 2
- enc_bias: float32 [40960], P('lat'), may hold values from -3 to 3
- dec_weight: bfloat16 [8, 40960, 2304], P('layer', 'lat'), may hold values from -0.03125 to 0.03125
- dec_scale: float32 [8, 320, 18], P('layer', 'lat'), may hold values from 0.5 to 2
- dec_bias: float32 [8, 2304], P('layer'), may hold values from -3 to 3
Outputs:
- recon: bfloat16 [8, 512, 2304], P('layer', 'lat')
- latents: bfloat16 [512, 40960], P(None, 'lat')
All inputs are finite; a program needn't handle non-finite values.
Results may differ from a plain program's by a relative error of at most 0.025.
Values may be sent and summed in bfloat16 or wider, within the bound.
No kernel may reach another device: no remote copies, remote signals or barrier semaphores. Data moves between devices by JAX's collectives and lax.ppermute only.
A program may use at most 64 MiB of HBM per device.

v0:
```python
import jax
import jax.numpy as jnp
from jax import lax
from jax.sharding import PartitionSpec as P

BLOCK = 128


def dequant(quant, scale):
    full = jnp.repeat(jnp.repeat(scale, BLOCK, axis=0), BLOCK, axis=1)
    return (quant.astype(jnp.float32) * full).astype(jnp.bfloat16)


def on_device(acts, enc_weight, enc_scale, enc_bias, dec_weight, dec_scale, dec_bias):
    enc_full = dequant(enc_weight[0], enc_scale[0])
    dec_full = dequant(dec_weight[0], dec_scale[0])
    local_rows = acts[0]
    terms = jnp.dot(
        lax.all_gather(local_rows, "lat", axis=0, tiled=True),
        enc_full,
        preferred_element_type=jnp.float32,
    )
    preact = lax.psum(terms.astype(jnp.bfloat16), "layer").astype(jnp.float32) + enc_bias[None, :]
    latents = jnp.maximum(preact, 0.0).astype(jnp.bfloat16)
    summed = lax.psum_scatter(
        jnp.dot(latents, dec_full, preferred_element_type=jnp.float32).astype(jnp.bfloat16),
        "lat",
        scatter_dimension=0,
        tiled=True,
    ).astype(jnp.float32)
    recon = (summed + dec_bias[0][None, :]).astype(jnp.bfloat16)
    return (recon[None], latents)


def solution(mesh):
    in_specs = (
        P("layer", "lat", None),
        P("layer", None, "lat"),
        P("layer", None, "lat"),
        P("lat"),
        P("layer", "lat", None),
        P("layer", "lat", None),
        P("layer", None),
    )
    out_specs = (P("layer", "lat", None), P(None, "lat"))
    return jax.shard_map(
        on_device, mesh=mesh, in_specs=in_specs, out_specs=out_specs, check_vma=False
    )
```

profile of v0, /device:TPU:8, one launch (start us, length us, event | category | flops | bytes accessed | tf_op | source)
XLA Modules:
  0.0 270.7 jit_solution(3056183138706317476)
XLA Ops:
  7.2 0.0 all-gather.3.cloned.1.call-start
  7.2 0.7 all-gather.3.cloned.1.call-update
  7.9 0.0 all-reduce.2.cloned.1.call-start
  8.0 8.8 %copy.15 = bf16[1,2304,1280]{1,2,0:T(8,128)(2,1)} copy(bf16[1,2304,1280]{2,1,0:T(8,128)(2,1)} %param.8) | data formatting | bytes 11796480 | tf_op args[1]
  16.8 0.1 broadcast_bitcast_fusion.1
  17.0 6.3 %fusion.1 = bf16[2304,1280]{0,1:T(8,128)(2,1)} fusion(bf16[1,2304,1280]{1,2,0:T(8,128)(2,1)} %copy.15, f32[2304,10]{0,1:T(8,128)S(1)} %bitcast.38), kind=kLoop, calls=%fused_computation.3 | loop fusion | flops 8847360 | bytes 11888640 | tf_op jit(solution)/shard_map/convert_element_type | solution.py:11
  23.3 45.6 %all-gather.3.cloned.1.call-done = bf16[1,512,2304]{2,1,0:T(8,128)(2,1)} async-done(((bf16[1,16,2304]{2,1,0:T(8,128)(2,1)}), bf16[1,512,2304]{2,1,0:T(8,128)(2,1)}) %all-gather.3.cloned.1.call-update) | async-done | bytes 2359312 | tf_op jit(solution)/shard_map/all_gather | solution.py:19
  68.9 7.7 %fusion.2 = bf16[512,1280]{0,1:T(8,128)(2,1)} fusion(bf16[2304,1280]{0,1:T(8,128)(2,1)} %fusion.1, bf16[1,512,2304]{2,1,0:T(8,128)(2,1)} %all-gather.3.cloned.1.call-done), kind=kOutput, calls=%fused_computation.6 | convolution fusion | flops 3020554240 | bytes 9568256 | tf_op jit(solution)/shard_map/dot_general | solution.py:18
  76.6 0.0 all-reduce.2.cloned.1.call-update
  76.6 0.0 copy-start.3
  76.6 0.0 reduce-scatter.2.cloned.1.call-start
  76.7 8.9 %copy.16 = bf16[1,1280,2304]{1,2,0:T(8,128)(2,1)} copy(bf16[1,1280,2304]{2,1,0:T(8,128)(2,1)} %param.11) | data formatting | bytes 11796480 | tf_op args[4]
  85.6 0.1 copy.19
  85.7 0.1 broadcast_bitcast_fusion
  85.8 0.0 copy-start.1
  85.9 6.3 %fusion = bf16[1280,2304]{0,1:T(8,128)(2,1)} fusion(bf16[1,1280,2304]{1,2,0:T(8,128)(2,1)} %copy.16, f32[1280,18]{0,1:T(8,128)S(1)} %bitcast.39), kind=kLoop, calls=%fused_computation.1 | loop fusion | flops 8847360 | bytes 11888640 | tf_op jit(solution)/shard_map/convert_element_type | solution.py:11
  92.2 68.3 %all-reduce.2.cloned.1.call-done = bf16[512,1280]{0,1:T(8,128)(2,1)} async-done(((bf16[512,1280]{0,1:T(8,128)(2,1)}), bf16[512,1280]{0,1:T(8,128)(2,1)}) %all-reduce.2.cloned.1.call-update) | async-done | bytes 1310736 | tf_op jit(solution)/shard_map/psum | solution.py:23
  160.5 1.7 maximum_convert_fusion
  162.1 0.0 copy-start
  162.2 7.2 %convolution_convert_fusion = bf16[512,2304]{1,0:T(8,128)(2,1)} fusion(bf16[512,1280]{0,1:T(8,128)(2,1)S(1)} %maximum_convert_fusion, bf16[1280,2304]{0,1:T(8,128)(2,1)} %fusion), kind=kOutput, calls=%fused_computation.4 | convolution fusion | flops 3021078528 | bytes 9568256 | tf_op jit(solution)/shard_map/dot_general | solution.py:26
  169.4 0.0 reduce-scatter.2.cloned.1.call-update
  169.5 1.4 copy.18
  170.9 91.7 %reduce-scatter.2.cloned.1.call-done = bf16[16,2304]{1,0:T(8,128)(2,1)} async-done(((bf16[512,2304]{1,0:T(8,128)(2,1)}), bf16[16,2304]{1,0:T(8,128)(2,1)}) %reduce-scatter.2.cloned.1.call-update) | async-done | bytes 73744 | tf_op jit(solution)/shard_map/reduce_scatter | solution.py:25
  262.6 1.5 fusion.4
  (11 shorter events, 0.1 us)
Async XLA Ops:
  7.2 61.7 %all-gather.3.cloned.1.call-start = ((), (), s32[]{:S(2)}) async-start(), calls=%async_computation.3 | async-start | bytes 2433024 | tf_op jit(solution)/shard_map/all_gather | solution.py:19
  7.9 8.9 %copy-start.2 = (f32[1,18,10]{1,0,2:T(1,128)S(1)}, f32[1,18,10]{1,0,2:T(1,128)}, u32[]{:S(2)}) copy-start(f32[1,18,10]{1,0,2:T(1,128)} %param.9) | copy-start | bytes 2164
  7.9 152.6 %all-reduce.2.cloned.1.call-start = ((), (), s32[]{:S(2)}) async-start(), calls=%async_computation.1 | async-start | bytes 2621440 | tf_op jit(solution)/shard_map/psum | solution.py:23
  76.6 9.0 %copy-start.3 = (f32[1,10,18]{2,0,1:T(1,128)S(1)}, f32[1,10,18]{2,0,1:T(1,128)}, u32[]{:S(2)}) copy-start(f32[1,10,18]{2,0,1:T(1,128)} %param.12) | copy-start | bytes 2164
  76.6 186.0 %reduce-scatter.2.cloned.1.call-start = ((), (), s32[]{:S(2)}) async-start(), calls=%async_computation.2 | async-start | bytes 2433024 | tf_op jit(solution)/shard_map/reduce_scatter | solution.py:25
  85.8 74.6 %copy-start.1 = (f32[1280]{0:T(1024)S(1)}, f32[1280]{0:T(1024)}, u32[]{:S(2)}) copy-start(f32[1280]{0:T(1024)} %param.10) | copy-start | bytes 15364
  162.1 7.3 %copy-start = (f32[1,2304]{1,0:T(1,128)S(1)}, f32[1,2304]{1,0:T(1,128)}, u32[]{:S(2)}) copy-start(f32[1,2304]{1,0:T(1,128)} %param.13) | copy-start | bytes 27652
Sparse Core Ops, SparseCore 0:
  10.5 58.2 all-gather.2
  76.7 83.7 all-reduce.1
  169.5 93.0 reduce-scatter.1
where the time goes:
time: 271 us
  waiting for transfers between devices  206 us (76%)
  local copies, waits for them, and re-layouts  19.6 us (7%)
  other arithmetic  15.9 us (6%)
  matrix products  14.9 us (5%)
  between operations  13.8 us (5%)
    reduce_scatter x1, waiting for transfers between devices, on_device(): lax.psum_scatter(jnp.dot(latents, dec_full, preferred_element_type=jnp.fl...  91.7 us
    psum x1, waiting for transfers between devices, on_device(): lax.psum(terms.astype(jnp.bfloat16), 'layer').astype(jnp.float32)  68.3 us
    all_gather x1, waiting for transfers between devices, on_device(): lax.all_gather(local_rows, 'lat', axis=0, tiled=True)  45.6 us
    unnamed x18, local copies, waits for them, and re-layouts  19.5 us
    convert_element_type x2, other arithmetic, dequant(): return (quant.astype(jnp.float32) * full).astype(jnp.bfloat16)  12.7 us
    dot_general x1, matrix products, on_device(): jnp.dot(lax.all_gather(local_rows, 'lat', axis=0, tiled=True), enc_full,...  7.7 us
    dot_general x1, matrix products, on_device(): jnp.dot(latents, dec_full, preferred_element_type=jnp.float32)  7.23 us
  transfers between devices with their start and end apart: 3, of which 3 were waited for; matrix products, arithmetic and copies ran while one was open for 12% of the time, Pallas kernels for 0%

commit v1 on v0

v1 whole, which is shorter than its diff:
```python
import functools

import jax
import jax.numpy as jnp
from jax import lax
from jax.experimental import pallas as pl
from jax.experimental.pallas import tpu as pltpu
from jax.sharding import Mesh, PartitionSpec as P

BLOCK = 128
Y, ZL, X, ZH, C = 4, 2, 4, 4, 2
LAYER, LAT = ("y", "zl"), ("x", "zh", "c")
F32, BF16 = jnp.float32, jnp.bfloat16
MIB = 1 << 20


def params(mib):
    return pltpu.CompilerParams(vmem_limit_bytes=mib * MIB)


def cost(flops, moved):
    return pl.CostEstimate(flops=flops, bytes_accessed=moved, transcendentals=0)


def dequant_kernel(scale_ref, w_ref, out_ref):
    step = pl.program_id(0)
    rows, columns = w_ref.shape
    for i in range(rows // BLOCK):
        for j in range(columns // BLOCK):
            at = (slice(i * BLOCK, (i + 1) * BLOCK), slice(j * BLOCK, (j + 1) * BLOCK))
            scale = scale_ref[step * (rows // BLOCK) + i, j]
            out_ref[at] = (w_ref[at].astype(F32) * scale).astype(BF16)


def dequant(weight, scale):
    depth, width = weight.shape
    rows = 2 * BLOCK
    return pl.pallas_call(
        dequant_kernel,
        grid=(depth // rows,),
        in_specs=[
            pl.BlockSpec(memory_space=pltpu.SMEM),
            pl.BlockSpec((rows, width), lambda i: (i, 0)),
        ],
        out_specs=pl.BlockSpec((rows, width), lambda i: (i, 0)),
        out_shape=jax.ShapeDtypeStruct((depth, width), BF16),
        compiler_params=params(16),
        cost_estimate=cost(depth * width, 4 * depth * width),
        name="dequant",
    )(scale, weight)


def encode_kernel(*refs):
    pieces, w_ref, out_ref, rows_ref = refs[:-3], refs[-3], refs[-2], refs[-1]
    height = pieces[0].shape[0]

    @pl.when(pl.program_id(0) == 0)
    def _():
        for k, piece in enumerate(pieces):
            rows_ref[k * height : (k + 1) * height, :] = piece[...]

    out_ref[...] = jnp.dot(rows_ref[...], w_ref[...], preferred_element_type=F32).astype(BF16)


def encode(pieces, weight):
    depth, width = weight.shape
    height = pieces[0].shape[0]
    total, tile = height * len(pieces), 256
    return pl.pallas_call(
        encode_kernel,
        grid=(width // tile,),
        in_specs=[pl.BlockSpec((height, depth), lambda i: (0, 0))] * len(pieces)
        + [pl.BlockSpec((depth, tile), lambda i: (0, i))],
        out_specs=pl.BlockSpec((total, tile), lambda i: (0, i)),
        out_shape=jax.ShapeDtypeStruct((total, width), BF16),
        scratch_shapes=[pltpu.VMEM((total, depth), BF16)],
        compiler_params=params(16),
        cost_estimate=cost(2 * total * depth * width, 2 * (depth * width + total * (depth + width))),
        name="encode",
    )(*pieces, weight)


def activate_kernel(terms_ref, bias_ref, out_ref):
    preact = jnp.sum(terms_ref[...].astype(F32), axis=0) + bias_ref[...]
    latents = jnp.maximum(preact, 0.0).astype(BF16)
    for m in range(out_ref.shape[0]):
        out_ref[m] = latents


def activate(terms, bias):
    members, height, width = terms.shape
    tile = 256
    return pl.pallas_call(
        activate_kernel,
        grid=(width // tile,),
        in_specs=[
            pl.BlockSpec((members, height, tile), lambda i: (0, 0, i)),
            pl.BlockSpec((1, tile), lambda i: (0, i)),
        ],
        out_specs=pl.BlockSpec((members, height, tile), lambda i: (0, 0, i)),
        out_shape=jax.ShapeDtypeStruct(terms.shape, BF16),
        compiler_params=params(16),
        cost_estimate=cost(terms.size, 4 * terms.size),
        name="activate",
    )(terms, bias)


def place_kernel(where_ref, latents_ref, out_ref, sem):
    x, zh, c = where_ref[0], where_ref[1], where_ref[2]
    height = 16
    copies = []
    for kc in range(C):
        for kx in range(X):
            for kz in range(ZH):
                b = (kc * X + kx) * ZH + kz
                owner = (((x + kx) % X) * ZH + (zh + kz) % ZH) * C + (c + kc) % C
                copies.append(
                    pltpu.make_async_copy(
                        latents_ref.at[pl.ds(b * height, height), :],
                        out_ref.at[pl.ds(pl.multiple_of(owner * height, height), height), :],
                        sem.at[b],
                    )
                )
    for copy in copies:
        copy.start()
    for copy in copies:
        copy.wait()


def place(where, latents):
    return pl.pallas_call(
        place_kernel,
        in_specs=[pl.BlockSpec(memory_space=pltpu.SMEM), pl.BlockSpec(memory_space=pl.ANY)],
        out_specs=pl.BlockSpec(memory_space=pl.ANY),
        out_shape=jax.ShapeDtypeStruct(latents.shape, BF16),
        scratch_shapes=[pltpu.SemaphoreType.DMA((C * X * ZH,))],
        compiler_params=params(4),
        cost_estimate=cost(0, 4 * latents.size),
        name="place",
    )(where, latents)


def decode_kernel(latents_ref, w_ref, out_ref):
    out_ref[...] = jnp.dot(latents_ref[...], w_ref[...], preferred_element_type=F32).astype(BF16)


def decode(latents, weight, half):
    depth, width = weight.shape
    total, tile = latents.shape[0] // 2, 256
    return pl.pallas_call(
        decode_kernel,
        grid=(width // tile,),
        in_specs=[
            pl.BlockSpec((total, depth), lambda i: (half, 0)),
            pl.BlockSpec((depth, tile), lambda i: (0, i)),
        ],
        out_specs=pl.BlockSpec((total, tile), lambda i: (0, i)),
        out_shape=jax.ShapeDtypeStruct((total, width), BF16),
        compiler_params=params(16),
        cost_estimate=cost(2 * total * depth * width, 2 * (depth * width + total * (depth + width))),
        name="decode",
    )(latents, weight)


def total_kernel(*refs, terms, bias):
    ins, outs = refs[: terms + bias], refs[terms + bias :]
    total = ins[0][...].astype(F32)
    for ref in ins[1:]:
        total = total + ref[...].astype(F32)
    height = outs[0].shape[0]
    for k, out in enumerate(outs):
        out[...] = total[k * height : (k + 1) * height].astype(BF16)


def total(arrays, cuts, bias=None):
    height, width = arrays[0].shape
    ins = list(arrays) + ([] if bias is None else [bias])
    out = jax.ShapeDtypeStruct((height // cuts, width), BF16)
    return pl.pallas_call(
        functools.partial(total_kernel, terms=len(arrays), bias=bias is not None),
        in_specs=[pl.BlockSpec(memory_space=pltpu.VMEM)] * len(ins),
        out_specs=[pl.BlockSpec(memory_space=pltpu.VMEM)] * cuts,
        out_shape=[out] * cuts,
        compiler_params=params(24),
        cost_estimate=cost(height * width, 2 * (len(arrays) + 1) * height * width),
        name="total",
    )(*ins)


def send(array, axis, size, by):
    return lax.ppermute(array, axis, [(i, (i + by) % size) for i in range(size)])


def on_device(acts, enc_weight, enc_scale, enc_bias, dec_weight, dec_scale, dec_bias):
    where = jnp.stack([lax.axis_index("x"), lax.axis_index("zh"), lax.axis_index("c")]).astype(jnp.int32)
    own = acts[0]
    column = jnp.concatenate([own] + [send(own, "zh", ZH, -k) for k in (1, 2, 3)], axis=0)
    mine = [column] + [send(column, "x", X, -k) for k in (1, 2, 3)]
    other = [send(piece, "c", C, 1) for piece in mine]
    enc_full = dequant(enc_weight[0], enc_scale[0])
    dec_full = dequant(dec_weight[0], dec_scale[0])
    terms = jnp.concatenate([encode(mine, enc_full), encode(other, enc_full)], axis=0)
    members = Y * ZL
    terms = terms.reshape(members, terms.shape[0] // members, terms.shape[1])
    terms = lax.all_to_all(terms, LAYER, 0, 0, tiled=True)
    copies = activate(terms, enc_bias[None, :])
    latents = lax.all_to_all(copies, LAYER, 0, 0, tiled=True)
    latents = latents.reshape(-1, latents.shape[-1])
    theirs = send(decode(latents, dec_full, 1), "c", C, 1)
    part = total([decode(latents, dec_full, 0), theirs], X)
    part = total([part[0]] + [send(part[k], "x", X, k) for k in (1, 2, 3)], ZH)
    recon = total([part[0]] + [send(part[k], "zh", ZH, k) for k in (1, 2, 3)], 1, dec_bias)[0]
    return (recon[None], place(where, latents))


def solution(mesh):
    axes = ("y", "zl", "x", "zh", "c")
    fine = Mesh(mesh.devices.reshape(Y, ZL, X, ZH, C), axes)
    in_specs = (
        P(LAYER, LAT, None),
        P(LAYER, None, LAT),
        P(LAYER, None, LAT),
        P(LAT),
        P(LAYER, LAT, None),
        P(LAYER, LAT, None),
        P(LAYER, None),
    )
    out_specs = (P(LAYER, LAT, None), P(None, LAT))
    return jax.shard_map(on_device, mesh=fine, in_specs=in_specs, out_specs=out_specs, check_vma=False)
```

time: 271 us -> 141 us (0.52)
  waiting for transfers between devices: 206 us -> 63.8 us
  starting transfers between devices: 0.12 us -> 38.2 us
  Pallas kernels: 0 us -> 22.7 us
  matrix products: 14.9 us -> 0 us
  other arithmetic: 15.9 us -> 2.12 us
  between operations: 13.8 us -> 0.8 us
  local copies, waits for them, and re-layouts: 19.6 us -> 11.3 us
    reduce_scatter x1 -> x0, waiting for transfers between devices: 91.7 us -> none  [on_device(): lax.psum_scatter(jnp.dot(latents, dec_full, preferred_element_type=jnp.fl...]
    psum x1 -> x0, waiting for transfers between devices: 68.3 us -> none  [on_device(): lax.psum(terms.astype(jnp.bfloat16), 'layer').astype(jnp.float32)]
    all_gather x1 -> x0, waiting for transfers between devices: 45.6 us -> none  [on_device(): lax.all_gather(local_rows, 'lat', axis=0, tiled=True)]
    ppermute x0 -> x17, waiting for transfers between devices: none -> 37.3 us  [send(): lax.ppermute(array, axis, [(i, (i + by) % size) for i in range(size)])]
    ppermute x0 -> x17, starting transfers between devices: none -> 27.8 us  [send(): lax.ppermute(array, axis, [(i, (i + by) % size) for i in range(size)])]
    all_to_all x0 -> x2, waiting for transfers between devices: none -> 26.6 us  [the longest x1 17.4 us: on_device(): terms = lax.all_to_all(terms, LAYER, 0, 0, tiled=True)]
    pallas_call x0 -> x11, Pallas kernels: none -> 22.7 us  [the longest x2 7.34 us: decode(): pl.pallas_call(decode_kernel, grid=(width // tile,), in_specs=[pl.BlockSp...]
    dot_general x2 -> x0, matrix products: 14.9 us -> none  [the longest x1 7.7 us: on_device(): jnp.dot(lax.all_gather(local_rows, 'lat', axis=0, tiled=True), enc_full,...]
  transfers between devices with their start and end apart: 3 -> 19, of which waited for: 3 -> 10; matrix products, arithmetic and copies ran while one was open for 12% -> 1% of each run, Pallas kernels for 0% -> 9%
where the time goes in v1:
time: 141 us; the launch traced here: 139 us
  waiting for transfers between devices  63.8 us (45%)
  starting transfers between devices  38.2 us (27%)
  Pallas kernels  22.7 us (16%)
  local copies, waits for them, and re-layouts  11.3 us (8%)
  other arithmetic  2.12 us (2%)
    ppermute x17, waiting for transfers between devices, send(): lax.ppermute(array, axis, [(i, (i + by) % size) for i in range(size)])  37.3 us
    ppermute x17, starting transfers between devices, send(): lax.ppermute(array, axis, [(i, (i + by) % size) for i in range(size)])  27.8 us
    all_to_all x1, waiting for transfers between devices, on_device(): terms = lax.all_to_all(terms, LAYER, 0, 0, tiled=True)  17.4 us
    unnamed x16, local copies, waits for them, and re-layouts  11.3 us
    all_to_all x1, waiting for transfers between devices, on_device(): latents = lax.all_to_all(copies, LAYER, 0, 0, tiled=True)  9.14 us
    pallas_call x2, Pallas kernels, decode(): pl.pallas_call(decode_kernel, grid=(width // tile,), in_specs=[pl.BlockSp...  7.34 us
    pallas_call x2, Pallas kernels, encode(): pl.pallas_call(encode_kernel, grid=(width // tile,), in_specs=[pl.BlockSp...  5.99 us
    all_to_all x1, starting transfers between devices, on_device(): latents = lax.all_to_all(copies, LAYER, 0, 0, tiled=True)  5.39 us
  transfers between devices with their start and end apart: 19, of which 10 were waited for; matrix products, arithmetic and copies ran while one was open for 1% of the time, Pallas kernels for 9%

profile of v1, /device:TPU:8, one launch (start us, length us, event | category | flops | bytes accessed | tf_op | source)
XLA Modules:
  0.0 139.0 jit_solution(8811883954381034789)
XLA Ops:
  0.6 3.3 %collective-permute-start.2 = (bf16[16,2304]{1,0:T(8,128)(2,1)}, bf16[16,2304]{1,0:T(8,128)(2,1)S(1)}, u32[]{:S(2)}, u32[]{:S(2)}) collective-permute-start(bf16[16,2304]{1,0:T(8,128)(2,1)} %bitcast.20), channel_id=1, source_target_pairs={{0,2},{2,4},{4,6},{6,0},{1,3},{3,5},{5,7},{7,1},{8,10},{10,12},{12... | collective-permute-start | bytes 221192 | tf_op jit(solution)/shard_map/ppermute | solution.py:191
  4.0 5.4 %collective-permute-start.1 = (bf16[16,2304]{1,0:T(8,128)(2,1)}, bf16[16,2304]{1,0:T(8,128)(2,1)S(1)}, u32[]{:S(2)}, u32[]{:S(2)}) collective-permute-start(bf16[16,2304]{1,0:T(8,128)(2,1)} %bitcast.21), channel_id=1, source_target_pairs={{0,4},{2,6},{4,0},{6,2},{1,5},{3,7},{5,1},{7,3},{8,12},{10,14},{12... | collective-permute-start | bytes 221192 | tf_op jit(solution)/shard_map/ppermute | solution.py:191
  9.4 2.7 %collective-permute-start = (bf16[16,2304]{1,0:T(8,128)(2,1)}, bf16[16,2304]{1,0:T(8,128)(2,1)S(1)}, u32[]{:S(2)}, u32[]{:S(2)}) collective-permute-start(bf16[16,2304]{1,0:T(8,128)(2,1)} %bitcast.22), channel_id=1, source_target_pairs={{0,6},{2,0},{4,2},{6,4},{1,7},{3,1},{5,3},{7,5},{8,14},{10,8},{12,... | collective-permute-start | bytes 221192 | tf_op jit(solution)/shard_map/ppermute | solution.py:191
  12.0 2.5 %collective-permute-done.1 = bf16[16,2304]{1,0:T(8,128)(2,1)S(1)} collective-permute-done((bf16[16,2304]{1,0:T(8,128)(2,1)}, bf16[16,2304]{1,0:T(8,128)(2,1)S(1)}, u32[]{:S(2)}, u32[]{:S(2)}) %collective-permute-start.1) | collective-permute-done | bytes 73760 | tf_op jit(solution)/shard_map/ppermute | solution.py:191
  14.5 2.6 %collective-permute-done = bf16[16,2304]{1,0:T(8,128)(2,1)S(1)} collective-permute-done((bf16[16,2304]{1,0:T(8,128)(2,1)}, bf16[16,2304]{1,0:T(8,128)(2,1)S(1)}, u32[]{:S(2)}, u32[]{:S(2)}) %collective-permute-start) | collective-permute-done | bytes 73760 | tf_op jit(solution)/shard_map/ppermute | solution.py:191
  18.0 2.8 %collective-permute-start.3 = (bf16[64,2304]{1,0:T(8,128)(2,1)S(1)}, bf16[64,2304]{1,0:T(8,128)(2,1)S(1)}, u32[]{:S(2)}, u32[]{:S(2)}) collective-permute-start(bf16[64,2304]{1,0:T(8,128)(2,1)S(1)} %pad_maximum_fusion.1.refs_0_), channel_id=1, source_target_pairs={{0,24},{8,0},{16,8},{24,16},{1,25},{9,1},{17,9},{25,17},{2,26},{10... | collective-permute-start | bytes 884744 | tf_op jit(solution)/shard_map/ppermute | solution.py:191
  22.6 11.1 %collective-permute-done.3.refs_1_ = bf16[64,2304]{1,0:T(8,128)(2,1)S(1)} collective-permute-done((bf16[64,2304]{1,0:T(8,128)(2,1)S(1)}, bf16[64,2304]{1,0:T(8,128)(2,1)S(1)}, u32[]{:S(2)}, u32[]{:S(2)}) %collective-permute-start.3) | collective-permute-done | bytes 294944 | tf_op jit(solution)/shard_map/ppermute | solution.py:191
  34.2 3.2 %collective-permute-done.5.refs_3_ = bf16[64,2304]{1,0:T(8,128)(2,1)S(1)} collective-permute-done((bf16[64,2304]{1,0:T(8,128)(2,1)S(1)}, bf16[64,2304]{1,0:T(8,128)(2,1)S(1)}, u32[]{:S(2)}, u32[]{:S(2)}) %collective-permute-start.5) | collective-permute-done | bytes 294944 | tf_op jit(solution)/shard_map/ppermute | solution.py:191
  38.1 2.7 %copy-done.3 = bf16[1,2304,1280]{2,1,0:T(8,128)(2,1)S(1)} copy-done((bf16[1,2304,1280]{2,1,0:T(8,128)(2,1)S(1)}, bf16[1,2304,1280]{2,1,0:T(8,128)(2,1)}, u32[]{:S(2)}) %copy-start.3) | copy-done | bytes 5898264
  42.9 3.0 %encode.2 = bf16[256,1280]{1,0:T(8,128)(2,1)S(1)} custom-call(bf16[64,2304]{1,0:T(8,128)(2,1)S(1)} %pad_maximum_fusion.1.refs_0_, bf16[64,2304]{1,0:T(8,128)(2,1)S(1)} %collective-permute-done.3.refs_1_, bf16[64,2304]{1,0:T(8,128)(2,1)S(1)} %collective-permute-done.4.refs_2_, bf16[64,2304]{1,0:T(8,128)(2,1)S(1)} %collective-permute-done.5.refs_3_, ...), custom_call_target="tpu_custom_call" | custom-call | flops 1509949440 | bytes 7733248 | tf_op jit(solution)/shard_map/encode/pallas_call | solution.py:69
  46.0 3.0 %encode.3 = bf16[256,1280]{1,0:T(8,128)(2,1)S(1)} custom-call(bf16[64,2304]{1,0:T(8,128)(2,1)S(1)} %collective-permute-done.6.refs_0_, bf16[64,2304]{1,0:T(8,128)(2,1)S(1)} %collective-permute-done.7.refs_1_, bf16[64,2304]{1,0:T(8,128)(2,1)S(1)} %collective-permute-done.8.refs_2_, bf16[64,2304]{1,0:T(8,128)(2,1)S(1)} %collective-permute-done.9.refs_3_, ...), custom_call_target="tpu_custom_call" | custom-call | flops 1509949440 | bytes 7733248 | tf_op jit(solution)/shard_map/encode/pallas_call | solution.py:69
  50.1 5.0 %all-to-all-start = ((bf16[8,64,1280]{2,1,0:T(8,128)(2,1)}), bf16[8,64,1280]{2,1,0:T(8,128)(2,1)S(1)}, u32[]{:S(2)}, u32[]{:S(2)}) async-start(bf16[8,64,1280]{2,1,0:T(8,128)(2,1)} %bitcast.3), calls=%async_computation | async-start | bytes 2621440 | tf_op jit(solution)/shard_map/all_to_all | solution.py:205
  55.2 17.4 %all-to-all-done.terms_ref = bf16[8,64,1280]{2,1,0:T(8,128)(2,1)S(1)} async-done(((bf16[8,64,1280]{2,1,0:T(8,128)(2,1)}), bf16[8,64,1280]{2,1,0:T(8,128)(2,1)S(1)}, u32[]{:S(2)}, u32[]{:S(2)}) %all-to-all-start) | async-done | bytes 1310752 | tf_op jit(solution)/shard_map/all_to_all | solution.py:205
  72.6 2.3 %activate.1 = bf16[8,64,1280]{2,1,0:T(8,128)(2,1)} custom-call(bf16[8,64,1280]{2,1,0:T(8,128)(2,1)S(1)} %all-to-all-done.terms_ref, f32[1,1280]{1,0:T(1,128)S(1)} %broadcast_in_dim.6.bias_ref), custom_call_target="tpu_custom_call" | custom-call | flops 655360 | bytes 2621440 | tf_op jit(solution)/shard_map/activate/pallas_call | solution.py:93
  74.9 5.4 %all-to-all-start.1 = ((bf16[8,64,1280]{2,1,0:T(8,128)(2,1)}), bf16[8,64,1280]{2,1,0:T(8,128)(2,1)S(1)}, u32[]{:S(2)}, u32[]{:S(2)}) async-start(bf16[8,64,1280]{2,1,0:T(8,128)(2,1)} %activate.1), calls=%async_computation.1 | async-start | bytes 2621440 | tf_op jit(solution)/shard_map/all_to_all | solution.py:207
  80.3 2.7 %copy-done.2 = bf16[1,1280,2304]{2,1,0:T(8,128)(2,1)S(1)} copy-done((bf16[1,1280,2304]{2,1,0:T(8,128)(2,1)S(1)}, bf16[1,1280,2304]{2,1,0:T(8,128)(2,1)}, u32[]{:S(2)}) %copy-start.2) | copy-done | bytes 5898264
  85.0 2.5 %copy-done = bf16[1280,2304]{1,0:T(8,128)(2,1)} copy-done((bf16[1280,2304]{1,0:T(8,128)(2,1)}, bf16[1280,2304]{1,0:T(8,128)(2,1)S(1)}, u32[]{:S(2)}) %copy-start) | copy-done | bytes 5898264
  87.5 9.1 %all-to-all-done.1 = bf16[8,64,1280]{2,1,0:T(8,128)(2,1)S(1)} async-done(((bf16[8,64,1280]{2,1,0:T(8,128)(2,1)}), bf16[8,64,1280]{2,1,0:T(8,128)(2,1)S(1)}, u32[]{:S(2)}, u32[]{:S(2)}) %all-to-all-start.1) | async-done | bytes 1310752 | tf_op jit(solution)/shard_map/all_to_all | solution.py:207
  96.6 2.7 %copy-done.1 = bf16[1280,2304]{1,0:T(8,128)(2,1)S(1)} copy-done((bf16[1280,2304]{1,0:T(8,128)(2,1)S(1)}, bf16[1280,2304]{1,0:T(8,128)(2,1)}, u32[]{:S(2)}) %copy-start.1) | copy-done | bytes 5898264
  99.3 3.7 %decode.3 = bf16[256,2304]{1,0:T(8,128)(2,1)S(1)} custom-call(bf16[512,1280]{1,0:T(8,128)(2,1)S(1)} %bitcast.13, bf16[1280,2304]{1,0:T(8,128)(2,1)S(1)} %copy-done.1), custom_call_target="tpu_custom_call" | custom-call | flops 1509949440 | bytes 7733248 | tf_op jit(solution)/shard_map/decode/pallas_call | solution.py:150
  103.1 3.7 %decode.2.refs_0_ = bf16[256,2304]{1,0:T(8,128)(2,1)S(1)} custom-call(bf16[512,1280]{1,0:T(8,128)(2,1)S(1)} %bitcast.14, bf16[1280,2304]{1,0:T(8,128)(2,1)S(1)} %copy-done.1), custom_call_target="tpu_custom_call" | custom-call | flops 1509949440 | bytes 7733248 | tf_op jit(solution)/shard_map/decode/pallas_call | solution.py:150
  110.6 13.5 %collective-permute-done.11.refs_1_ = bf16[64,2304]{1,0:T(8,128)(2,1)S(1)} collective-permute-done((bf16[64,2304]{1,0:T(8,128)(2,1)S(1)}, bf16[64,2304]{1,0:T(8,128)(2,1)S(1)}, u32[]{:S(2)}, u32[]{:S(2)}) %collective-permute-start.11) | collective-permute-done | bytes 294944 | tf_op jit(solution)/shard_map/ppermute | solution.py:191
  125.7 4.9 %collective-permute-start.15 = (bf16[16,2304]{1,0:T(8,128)(2,1)S(1)}, bf16[16,2304]{1,0:T(8,128)(2,1)S(1)}, u32[]{:S(2)}, u32[]{:S(2)}) collective-permute-start(bf16[16,2304]{1,0:T(8,128)(2,1)S(1)} %get-tuple-element.16), channel_id=1, source_target_pairs={{0,4},{2,6},{4,0},{6,2},{1,5},{3,7},{5,1},{7,3},{8,12},{10,14},{12... | collective-permute-start | bytes 221192 | tf_op jit(solution)/shard_map/ppermute | solution.py:191
  135.9 2.3 %collective-permute-done.16.refs_3_ = bf16[16,2304]{1,0:T(8,128)(2,1)S(1)} collective-permute-done((bf16[16,2304]{1,0:T(8,128)(2,1)S(1)}, bf16[16,2304]{1,0:T(8,128)(2,1)S(1)}, u32[]{:S(2)}, u32[]{:S(2)}) %collective-permute-start.16) | collective-permute-done | bytes 73760 | tf_op jit(solution)/shard_map/ppermute | solution.py:191
  (45 shorter events, 20.7 us)
Async XLA Ops:
  0.6 11.4 %collective-permute-start.2 = (bf16[16,2304]{1,0:T(8,128)(2,1)}, bf16[16,2304]{1,0:T(8,128)(2,1)S(1)}, u32[]{:S(2)}, u32[]{:S(2)}) collective-permute-start(bf16[16,2304]{1,0:T(8,128)(2,1)} %bitcast.20), channel_id=1, source_target_pairs={{0,2},{2,4},{4,6},{6,0},{1,3},{3,5},{5,7},{7,1},{8,10},{10,12},{12... | collective-permute-start | bytes 221192 | tf_op jit(solution)/shard_map/ppermute | solution.py:191
  4.0 10.5 %collective-permute-start.1 = (bf16[16,2304]{1,0:T(8,128)(2,1)}, bf16[16,2304]{1,0:T(8,128)(2,1)S(1)}, u32[]{:S(2)}, u32[]{:S(2)}) collective-permute-start(bf16[16,2304]{1,0:T(8,128)(2,1)} %bitcast.21), channel_id=1, source_target_pairs={{0,4},{2,6},{4,0},{6,2},{1,5},{3,7},{5,1},{7,3},{8,12},{10,14},{12... | collective-permute-start | bytes 221192 | tf_op jit(solution)/shard_map/ppermute | solution.py:191
  9.4 7.8 %collective-permute-start = (bf16[16,2304]{1,0:T(8,128)(2,1)}, bf16[16,2304]{1,0:T(8,128)(2,1)S(1)}, u32[]{:S(2)}, u32[]{:S(2)}) collective-permute-start(bf16[16,2304]{1,0:T(8,128)(2,1)} %bitcast.22), channel_id=1, source_target_pairs={{0,6},{2,0},{4,2},{6,4},{1,7},{3,1},{5,3},{7,5},{8,14},{10,8},{12,... | collective-permute-start | bytes 221192 | tf_op jit(solution)/shard_map/ppermute | solution.py:191
  18.0 15.6 %collective-permute-start.3 = (bf16[64,2304]{1,0:T(8,128)(2,1)S(1)}, bf16[64,2304]{1,0:T(8,128)(2,1)S(1)}, u32[]{:S(2)}, u32[]{:S(2)}) collective-permute-start(bf16[64,2304]{1,0:T(8,128)(2,1)S(1)} %pad_maximum_fusion.1.refs_0_), channel_id=1, source_target_pairs={{0,24},{8,0},{16,8},{24,16},{1,25},{9,1},{17,9},{25,17},{2,26},{10... | collective-permute-start | bytes 884744 | tf_op jit(solution)/shard_map/ppermute | solution.py:191
  20.9 12.8 %collective-permute-start.4 = (bf16[64,2304]{1,0:T(8,128)(2,1)S(1)}, bf16[64,2304]{1,0:T(8,128)(2,1)S(1)}, u32[]{:S(2)}, u32[]{:S(2)}) collective-permute-start(bf16[64,2304]{1,0:T(8,128)(2,1)S(1)} %pad_maximum_fusion.1.refs_0_), channel_id=1, source_target_pairs={{0,16},{8,24},{16,0},{24,8},{1,17},{9,25},{17,1},{25,9},{2,18},{10... | collective-permute-start | bytes 884744 | tf_op jit(solution)/shard_map/ppermute | solution.py:191
  21.7 15.7 %collective-permute-start.5 = (bf16[64,2304]{1,0:T(8,128)(2,1)S(1)}, bf16[64,2304]{1,0:T(8,128)(2,1)S(1)}, u32[]{:S(2)}, u32[]{:S(2)}) collective-permute-start(bf16[64,2304]{1,0:T(8,128)(2,1)S(1)} %pad_maximum_fusion.1.refs_0_), channel_id=1, source_target_pairs={{0,8},{8,16},{16,24},{24,0},{1,9},{9,17},{17,25},{25,1},{2,10},{10... | collective-permute-start | bytes 884744 | tf_op jit(solution)/shard_map/ppermute | solution.py:191
  22.6 23.4 %collective-permute-start.6 = (bf16[64,2304]{1,0:T(8,128)(2,1)S(1)}, bf16[64,2304]{1,0:T(8,128)(2,1)S(1)}, u32[]{:S(2)}, u32[]{:S(2)}) collective-permute-start(bf16[64,2304]{1,0:T(8,128)(2,1)S(1)} %pad_maximum_fusion.1.refs_0_), channel_id=1, source_target_pairs={{0,1},{1,0},{2,3},{3,2},{4,5},{5,4},{6,7},{7,6},{8,9},{9,8},{10,11... | collective-permute-start | bytes 884744 | tf_op jit(solution)/shard_map/ppermute | solution.py:191
  33.7 12.3 %collective-permute-start.7 = (bf16[64,2304]{1,0:T(8,128)(2,1)S(1)}, bf16[64,2304]{1,0:T(8,128)(2,1)S(1)}, u32[]{:S(2)}, u32[]{:S(2)}) collective-permute-start(bf16[64,2304]{1,0:T(8,128)(2,1)S(1)} %collective-permute-done.3.refs_1_), channel_id=1, source_target_pairs={{0,1},{1,0},{2,3},{3,2},{4,5},{5,4},{6,7},{7,6},{8,9},{9,8},{10,11... | collective-permute-start | bytes 884744 | tf_op jit(solution)/shard_map/ppermute | solution.py:191
  33.7 12.3 %collective-permute-start.8 = (bf16[64,2304]{1,0:T(8,128)(2,1)S(1)}, bf16[64,2304]{1,0:T(8,128)(2,1)S(1)}, u32[]{:S(2)}, u32[]{:S(2)}) collective-permute-start(bf16[64,2304]{1,0:T(8,128)(2,1)S(1)} %collective-permute-done.4.refs_2_), channel_id=1, source_target_pairs={{0,1},{1,0},{2,3},{3,2},{4,5},{5,4},{6,7},{7,6},{8,9},{9,8},{10,11... | collective-permute-start | bytes 884744 | tf_op jit(solution)/shard_map/ppermute | solution.py:191
  37.3 8.6 %collective-permute-start.9 = (bf16[64,2304]{1,0:T(8,128)(2,1)S(1)}, bf16[64,2304]{1,0:T(8,128)(2,1)S(1)}, u32[]{:S(2)}, u32[]{:S(2)}) collective-permute-start(bf16[64,2304]{1,0:T(8,128)(2,1)S(1)} %collective-permute-done.5.refs_3_), channel_id=1, source_target_pairs={{0,1},{1,0},{2,3},{3,2},{4,5},{5,4},{6,7},{7,6},{8,9},{9,8},{10,11... | collective-permute-start | bytes 884744 | tf_op jit(solution)/shard_map/ppermute | solution.py:191
  50.1 5.1 %copy-start.5 = (f32[1280]{0:T(1024)S(1)}, f32[1280]{0:T(1024)}, u32[]{:S(2)}) copy-start(f32[1280]{0:T(1024)} %param.10) | copy-start | bytes 15364
  50.1 22.5 %all-to-all-start = ((bf16[8,64,1280]{2,1,0:T(8,128)(2,1)}), bf16[8,64,1280]{2,1,0:T(8,128)(2,1)S(1)}, u32[]{:S(2)}, u32[]{:S(2)}) async-start(bf16[8,64,1280]{2,1,0:T(8,128)(2,1)} %bitcast.3), calls=%async_computation | async-start | bytes 2621440 | tf_op jit(solution)/shard_map/all_to_all | solution.py:205
  74.9 5.4 %copy-start.6 = (f32[1,10,18]{2,0,1:T(1,128)S(1)}, f32[1,10,18]{2,0,1:T(1,128)}, u32[]{:S(2)}) copy-start(f32[1,10,18]{2,0,1:T(1,128)} %param.12) | copy-start | bytes 2164
  74.9 21.7 %all-to-all-start.1 = ((bf16[8,64,1280]{2,1,0:T(8,128)(2,1)}), bf16[8,64,1280]{2,1,0:T(8,128)(2,1)S(1)}, u32[]{:S(2)}, u32[]{:S(2)}) async-start(bf16[8,64,1280]{2,1,0:T(8,128)(2,1)} %activate.1), calls=%async_computation.1 | async-start | bytes 2621440 | tf_op jit(solution)/shard_map/all_to_all | solution.py:207
  80.3 2.7 %copy-start.2 = (bf16[1,1280,2304]{2,1,0:T(8,128)(2,1)S(1)}, bf16[1,1280,2304]{2,1,0:T(8,128)(2,1)}, u32[]{:S(2)}) copy-start(bf16[1,1280,2304]{2,1,0:T(8,128)(2,1)} %param.11) | copy-start | bytes 17694724
  96.6 2.7 %copy-start.1 = (bf16[1280,2304]{1,0:T(8,128)(2,1)S(1)}, bf16[1280,2304]{1,0:T(8,128)(2,1)}, u32[]{:S(2)}) copy-start(bf16[1280,2304]{1,0:T(8,128)(2,1)} %copy-done) | copy-start | bytes 17694724
  103.0 3.8 %collective-permute-start.10 = (bf16[256,2304]{1,0:T(8,128)(2,1)S(1)}, bf16[256,2304]{1,0:T(8,128)(2,1)S(1)}, u32[]{:S(2)}, u32[]{:S(2)}) collective-permute-start(bf16[256,2304]{1,0:T(8,128)(2,1)S(1)} %decode.3), channel_id=1, source_target_pairs={{0,1},{1,0},{2,3},{3,2},{4,5},{5,4},{6,7},{7,6},{8,9},{9,8},{10,11... | collective-permute-start | bytes 3538952 | tf_op jit(solution)/shard_map/ppermute | solution.py:191
  107.0 17.0 %collective-permute-start.11 = (bf16[64,2304]{1,0:T(8,128)(2,1)S(1)}, bf16[64,2304]{1,0:T(8,128)(2,1)S(1)}, u32[]{:S(2)}, u32[]{:S(2)}) collective-permute-start(bf16[64,2304]{1,0:T(8,128)(2,1)S(1)} %get-tuple-element.11), channel_id=1, source_target_pairs={{0,8},{8,16},{16,24},{24,0},{1,9},{9,17},{17,25},{25,1},{2,10},{10... | collective-permute-start | bytes 884744 | tf_op jit(solution)/shard_map/ppermute | solution.py:191
  107.1 16.9 %collective-permute-start.12 = (bf16[64,2304]{1,0:T(8,128)(2,1)S(1)}, bf16[64,2304]{1,0:T(8,128)(2,1)S(1)}, u32[]{:S(2)}, u32[]{:S(2)}) collective-permute-start(bf16[64,2304]{1,0:T(8,128)(2,1)S(1)} %get-tuple-element.12), channel_id=1, source_target_pairs={{0,16},{8,24},{16,0},{24,8},{1,17},{9,25},{17,1},{25,9},{2,18},{10... | collective-permute-start | bytes 884744 | tf_op jit(solution)/shard_map/ppermute | solution.py:191
  109.2 15.5 %collective-permute-start.13 = (bf16[64,2304]{1,0:T(8,128)(2,1)S(1)}, bf16[64,2304]{1,0:T(8,128)(2,1)S(1)}, u32[]{:S(2)}, u32[]{:S(2)}) collective-permute-start(bf16[64,2304]{1,0:T(8,128)(2,1)S(1)} %get-tuple-element.13), channel_id=1, source_target_pairs={{0,24},{8,0},{16,8},{24,16},{1,25},{9,1},{17,9},{25,17},{2,26},{10... | collective-permute-start | bytes 884744 | tf_op jit(solution)/shard_map/ppermute | solution.py:191
  124.8 9.7 %collective-permute-start.14 = (bf16[16,2304]{1,0:T(8,128)(2,1)S(1)}, bf16[16,2304]{1,0:T(8,128)(2,1)S(1)}, u32[]{:S(2)}, u32[]{:S(2)}) collective-permute-start(bf16[16,2304]{1,0:T(8,128)(2,1)S(1)} %get-tuple-element.15), channel_id=1, source_target_pairs={{0,2},{2,4},{4,6},{6,0},{1,3},{3,5},{5,7},{7,1},{8,10},{10,12},{12... | collective-permute-start | bytes 221192 | tf_op jit(solution)/shard_map/ppermute | solution.py:191
  125.7 10.2 %collective-permute-start.15 = (bf16[16,2304]{1,0:T(8,128)(2,1)S(1)}, bf16[16,2304]{1,0:T(8,128)(2,1)S(1)}, u32[]{:S(2)}, u32[]{:S(2)}) collective-permute-start(bf16[16,2304]{1,0:T(8,128)(2,1)S(1)} %get-tuple-element.16), channel_id=1, source_target_pairs={{0,4},{2,6},{4,0},{6,2},{1,5},{3,7},{5,1},{7,3},{8,12},{10,14},{12... | collective-permute-start | bytes 221192 | tf_op jit(solution)/shard_map/ppermute | solution.py:191
  130.6 7.7 %collective-permute-start.16 = (bf16[16,2304]{1,0:T(8,128)(2,1)S(1)}, bf16[16,2304]{1,0:T(8,128)(2,1)S(1)}, u32[]{:S(2)}, u32[]{:S(2)}) collective-permute-start(bf16[16,2304]{1,0:T(8,128)(2,1)S(1)} %get-tuple-element.17), channel_id=1, source_target_pairs={{0,6},{2,0},{4,2},{6,4},{1,7},{3,1},{5,3},{7,5},{8,14},{10,8},{12,... | collective-permute-start | bytes 221192 | tf_op jit(solution)/shard_map/ppermute | solution.py:191
  132.6 5.6 %copy-start.4 = (f32[1,2304]{1,0:T(1,128)S(1)}, f32[1,2304]{1,0:T(1,128)}, u32[]{:S(2)}) copy-start(f32[1,2304]{1,0:T(1,128)} %refs_4_.1) | copy-start | bytes 27652
  (2 other events, 5.2 us)

commit v2 on v0

v2 whole, which is shorter than its diff:
```python
import functools

import jax
import jax.numpy as jnp
from jax import lax
from jax.experimental import pallas as pl
from jax.experimental.pallas import tpu as pltpu
from jax.sharding import Mesh, PartitionSpec as P

BLOCK = 128
Y, ZL, X, ZH, C = 4, 2, 4, 4, 2
LAYER, LAT = ("y", "zl"), ("x", "zh", "c")
AROUND = (1, 3, 2)
F32, BF16 = jnp.float32, jnp.bfloat16
MIB = 1 << 20
IN_VMEM = pl.BlockSpec(memory_space=pltpu.VMEM)
IN_SMEM = pl.BlockSpec(memory_space=pltpu.SMEM)
ANYWHERE = pl.BlockSpec(memory_space=pl.ANY)


def params(mib):
    return pltpu.CompilerParams(vmem_limit_bytes=mib * MIB)


def cost(flops, moved):
    return pl.CostEstimate(flops=flops, bytes_accessed=moved, transcendentals=0)


def shape(*dims):
    return jax.ShapeDtypeStruct(dims, BF16)


def whole(kernel, ins, outs, name, flops=0, mib=16, where=None):
    moved = sum(a.size * a.dtype.itemsize for a in list(ins) + list(outs))
    place = [] if where is None else [where]
    return pl.pallas_call(
        kernel,
        in_specs=[IN_SMEM] * len(place) + [IN_VMEM] * len(ins),
        out_specs=[IN_VMEM] * len(outs),
        out_shape=list(outs),
        compiler_params=params(mib),
        cost_estimate=cost(flops, moved),
        name=name,
    )(*place, *ins)


def dequant_kernel(scale_ref, w_ref, out_ref, raw_ref, sem, *, by_row):
    rows, width = out_ref.shape
    step, steps = pl.program_id(0), raw_ref.shape[0] // rows

    def read(step):
        at = pl.ds(pl.multiple_of(step * rows, rows), rows)
        return pltpu.make_async_copy(w_ref.at[at, :], raw_ref.at[at, :], sem.at[step])

    @pl.when(step == 0)
    def _():
        for k in range(steps):
            read(k).start()

    read(step).wait()
    for i in range(rows // BLOCK):
        at = pl.ds(pl.multiple_of(step * rows + i * BLOCK, BLOCK), BLOCK)
        for j in range(width // BLOCK):
            columns = slice(j * BLOCK, (j + 1) * BLOCK)
            k = step * (rows // BLOCK) + i
            scale = scale_ref[k, 0, j] if by_row else scale_ref[j, 0, k]
            out_ref[i * BLOCK : (i + 1) * BLOCK, columns] = (raw_ref[at, columns].astype(F32) * scale).astype(BF16)


def dequant(weight, scale, rows, by_row):
    depth, width = weight.shape
    return pl.pallas_call(
        functools.partial(dequant_kernel, by_row=by_row),
        grid=(depth // rows,),
        in_specs=[IN_SMEM, ANYWHERE],
        out_specs=pl.BlockSpec((rows, width), lambda i: (i, 0)),
        out_shape=shape(depth, width),
        scratch_shapes=[pltpu.VMEM((depth, width), BF16), pltpu.SemaphoreType.DMA((depth // rows,))],
        compiler_params=params(16),
        cost_estimate=cost(depth * width, 4 * depth * width),
        name="dequant",
    )(scale, pltpu.with_memory_space_constraint(weight, pltpu.HBM))


def product(rows, w_ref, store, width=256):
    for j in range(w_ref.shape[1] // width):
        at = slice(j * width, (j + 1) * width)
        store(at, jnp.dot(rows, w_ref[:, at], preferred_element_type=F32).astype(BF16))


def encode_kernel(where_ref, mine_ref, theirs_ref, w_ref, *refs):
    outs, all_ref = refs[:Y], refs[Y]
    height = outs[0].shape[0]
    y = where_ref[0]
    rows = jnp.concatenate([mine_ref[...], theirs_ref[...]], axis=0)

    def store(at, tile):
        all_ref[:, at] = tile

    product(rows, w_ref, store)
    for r, out in enumerate(outs):
        quarter = lax.rem(y + r, Y)
        out[...] = all_ref[pl.ds(pl.multiple_of(quarter * height, height), height), :]


def encode(where, mine, theirs, weight):
    depth, width = weight.shape
    rows = mine.shape[0] + theirs.shape[0]
    return pl.pallas_call(
        encode_kernel,
        in_specs=[IN_SMEM] + [IN_VMEM] * 3,
        out_specs=[IN_VMEM] * Y,
        out_shape=[shape(rows // Y, width)] * Y,
        scratch_shapes=[pltpu.VMEM((rows, width), BF16)],
        compiler_params=params(16),
        cost_estimate=cost(2 * rows * depth * width, 2 * depth * width),
        name="encode",
    )(where, mine, theirs, weight)


def decode_kernel(where_ref, *refs):
    quarters, w_ref, mine_ref, theirs_ref, all_ref = refs[:Y], refs[Y], refs[Y + 1], refs[Y + 2], refs[Y + 3]
    height, half = quarters[0].shape[0], mine_ref.shape[0]
    y = where_ref[0]
    for r, ref in enumerate(quarters):
        quarter = lax.rem(y + r, Y)
        all_ref[pl.ds(pl.multiple_of(quarter * height, height), height), :] = ref[...]

    def store(at, tile):
        mine_ref[:, at] = tile[:half]
        theirs_ref[:, at] = tile[half:]

    product(all_ref[...], w_ref, store)


def decode(where, quarters, weight):
    depth, width = weight.shape
    rows = quarters[0].shape[0] * Y
    return pl.pallas_call(
        decode_kernel,
        in_specs=[IN_SMEM] + [IN_VMEM] * (Y + 1),
        out_specs=[IN_VMEM] * 2,
        out_shape=[shape(rows // 2, width)] * 2,
        scratch_shapes=[pltpu.VMEM((rows, depth), BF16)],
        compiler_params=params(16),
        cost_estimate=cost(2 * rows * depth * width, 2 * depth * width),
        name="decode",
    )(where, *quarters, weight)


def join_kernel(*refs):
    height = refs[0].shape[0]
    for k, ref in enumerate(refs[:-1]):
        refs[-1][k * height : (k + 1) * height, :] = ref[...]


def sum_kernel(*refs, terms):
    ins, outs = refs[:terms], refs[terms:]
    height = outs[0].shape[0]
    for k, out in enumerate(outs):
        at = slice(k * height, (k + 1) * height)
        total = ins[0][at, :].astype(F32)
        for ref in ins[1:]:
            total = total + ref[at, :].astype(F32)
        out[...] = total.astype(BF16)


def added(arrays, cuts, name):
    rows, width = arrays[0].shape
    return whole(
        functools.partial(sum_kernel, terms=len(arrays)), arrays, [shape(rows // cuts, width)] * cuts, name
    )


def activate_kernel(a_ref, b_ref, bias_ref, out_ref):
    preact = (a_ref[...].astype(F32) + b_ref[...].astype(F32)) + bias_ref[...].reshape(1, -1)
    out_ref[...] = jnp.maximum(preact, 0.0).astype(BF16)


def finish_kernel(*refs):
    total = refs[-2][...]
    for ref in refs[:-2]:
        total = total + ref[...].astype(F32)
    refs[-1][...] = total.astype(BF16)


def place_kernel(where_ref, *refs):
    latents, out_ref, sem = refs[:-2], refs[-2], refs[-1]
    y, x, zh, c = (where_ref[i] for i in range(4))
    height = 16
    blocks = latents[0].shape[0] // height
    copies = []
    for a, ref in enumerate(latents):
        n, quarter = a // Y, lax.rem(y + a % Y, Y)
        for j in range(blocks):
            b = quarter * blocks + j
            kc, kx, k = b // (2 * X), lax.rem(b // 2, X), lax.rem(b, 2)
            owner = (lax.rem(x + kx, X) * ZH + lax.rem(zh + 2 * (1 - n) + k, ZH)) * C + lax.rem(c + kc, C)
            copies.append(
                pltpu.make_async_copy(
                    ref.at[pl.ds(j * height, height), :],
                    out_ref.at[pl.ds(pl.multiple_of(owner * height, height), height), :],
                    sem.at[a * blocks + j],
                )
            )
    for copy in copies:
        copy.start()
    for copy in copies:
        copy.wait()


def place(where, latents):
    rows, width = latents[0].shape
    rows *= len(latents)
    return pl.pallas_call(
        place_kernel,
        in_specs=[IN_SMEM] + [ANYWHERE] * len(latents),
        out_specs=ANYWHERE,
        out_shape=shape(rows, width),
        scratch_shapes=[pltpu.SemaphoreType.DMA((rows // 16,))],
        compiler_params=params(4),
        cost_estimate=cost(0, 4 * rows * width),
        name="place",
    )(where, *latents)


def after(array, *others):
    return lax.optimization_barrier((array,) + others)[0]


def send(array, axis, size, by):
    return lax.ppermute(array, axis, [(i, (i + by) % size) for i in range(size)])


def fetch_around(array, axis, size):
    got = {k: send(array, axis, size, -k) for k in AROUND}
    return [array] + [got[k] for k in (1, 2, 3)]


def hand_around(arrays, axis, size):
    return [arrays[0]] + [send(arrays[k], axis, size, k) for k in AROUND]


def on_device(acts, enc_weight, enc_scale, enc_bias, dec_weight, dec_scale, dec_bias):
    depth, width = enc_weight.shape[1:]
    own = acts[0]
    rows = own.shape[0]
    chunk = 2 * rows
    where = jnp.stack([lax.axis_index(a) for a in ("y", "x", "zh", "c")]).astype(jnp.int32)
    near, far, back = (send(own, "zh", ZH, -k) for k in (1, 2, 3))
    enc_full = dequant(enc_weight[0], after(jnp.transpose(enc_scale, (2, 0, 1)), where), 2 * BLOCK, False)
    pairs = ([far, after(back, enc_full, near)], [own, near])
    quarters, pieces, terms = [], None, None
    for n, pair in enumerate(pairs):
        if n == 1:
            pair[1] = after(pair[1], pieces[1])
        column = whole(join_kernel, pair, [shape(chunk, depth)], "join")[0]
        pieces = fetch_around(column, "x", X)
        if n == 1:
            pieces[1] = after(pieces[1], terms[0])
        mine = whole(join_kernel, pieces, [shape(X * chunk, depth)], "join")[0]
        theirs = send(mine, "c", C, 1)
        terms = list(encode(where, mine, theirs, enc_full))
        if n == 0:
            dec_full = dequant(dec_weight[0], after(jnp.transpose(dec_scale, (1, 0, 2)), terms[0]), BLOCK, True)
            terms[0] = after(terms[0], dec_full)
        part = added(hand_around(terms, "y", Y), 1, "gather")[0]
        latents = whole(activate_kernel, [part, send(part, "zl", ZL, 1), enc_bias], [shape(*part.shape)], "activate")[0]
        quarters.append(fetch_around(latents, "y", Y))
    parts, done = [], None
    for n in range(2):
        latents = list(quarters[n])
        if done is not None:
            latents[0] = after(latents[0], done)
        mine, theirs = decode(where, latents, dec_full)
        done = mine
        cuts = added([mine, send(theirs, "c", C, 1)], X, "add")
        low, high = added(hand_around(cuts, "x", X), 2, "fold")
        parts += [send(low, "zh", ZH, 2), send(high, "zh", ZH, 3)] if n == 0 else [low, send(high, "zh", ZH, 1)]
    recon = whole(finish_kernel, parts + [dec_bias], [shape(rows, depth)], "finish")[0]
    return (recon[None], place(where, quarters[0] + quarters[1]))


def solution(mesh):
    axes = ("y", "zl", "x", "zh", "c")
    fine = Mesh(mesh.devices.reshape(Y, ZL, X, ZH, C), axes)
    in_specs = (
        P(LAYER, LAT, None),
        P(LAYER, None, LAT),
        P(LAYER, None, LAT),
        P(LAT),
        P(LAYER, LAT, None),
        P(LAYER, LAT, None),
        P(LAYER, None),
    )
    out_specs = (P(LAYER, LAT, None), P(None, LAT))
    return jax.shard_map(on_device, mesh=fine, in_specs=in_specs, out_specs=out_specs, check_vma=False)
```

time: 271 us -> 108 us (0.40)
  waiting for transfers between devices: 206 us -> 27.1 us
  starting transfers between devices: 0.12 us -> 57.9 us
  Pallas kernels: 0 us -> 19.6 us
  local copies, waits for them, and re-layouts: 19.6 us -> 0.71 us
  other arithmetic: 15.9 us -> 0.08 us
  matrix products: 14.9 us -> 0 us
  between operations: 13.8 us -> 0.92 us
    reduce_scatter x1 -> x0, waiting for transfers between devices: 91.7 us -> none  [on_device(): lax.psum_scatter(jnp.dot(latents, dec_full, preferred_element_type=jnp.fl...]
    psum x1 -> x0, waiting for transfers between devices: 68.3 us -> none  [on_device(): lax.psum(terms.astype(jnp.bfloat16), 'layer').astype(jnp.float32)]
    ppermute x0 -> x36, starting transfers between devices: none -> 57.9 us  [send(): lax.ppermute(array, axis, [(i, (i + by) % size) for i in range(size)])]
    all_gather x1 -> x0, waiting for transfers between devices: 45.6 us -> none  [on_device(): lax.all_gather(local_rows, 'lat', axis=0, tiled=True)]
    ppermute x0 -> x36, waiting for transfers between devices: none -> 27.1 us  [send(): lax.ppermute(array, axis, [(i, (i + by) % size) for i in range(size)])]
    pallas_call x0 -> x20, Pallas kernels: none -> 19.6 us  [the longest x2 7.02 us: dequant(): pl.pallas_call(functools.partial(dequant_kernel, by_row=by_row), grid=(de...]
    unnamed x18 -> x10, local copies, waits for them, and re-layouts: 19.5 us -> 0.71 us
    dot_general x2 -> x0, matrix products: 14.9 us -> none  [the longest x1 7.7 us: on_device(): jnp.dot(lax.all_gather(local_rows, 'lat', axis=0, tiled=True), enc_full,...]
  transfers between devices with their start and end apart: 3 -> 36, of which waited for: 3 -> 13; matrix products, arithmetic and copies ran while one was open for 12% -> 0% of each run, Pallas kernels for 0% -> 18%
where the time goes in v2:
time: 108 us; the launch traced here: 106 us
  starting transfers between devices  57.9 us (54%)
  waiting for transfers between devices  27.1 us (25%)
  Pallas kernels  19.6 us (18%)
    ppermute x36, starting transfers between devices, send(): lax.ppermute(array, axis, [(i, (i + by) % size) for i in range(size)])  57.9 us
    ppermute x36, waiting for transfers between devices, send(): lax.ppermute(array, axis, [(i, (i + by) % size) for i in range(size)])  27.1 us
    pallas_call x2, Pallas kernels, dequant(): pl.pallas_call(functools.partial(dequant_kernel, by_row=by_row), grid=(de...  7.02 us
    pallas_call x2, Pallas kernels, decode(): pl.pallas_call(decode_kernel, in_specs=[IN_SMEM] + [IN_VMEM] * (Y + 1), o...  4.61 us
    pallas_call x2, Pallas kernels, encode(): pl.pallas_call(encode_kernel, in_specs=[IN_SMEM] + [IN_VMEM] * 3, out_spe...  4.56 us
  transfers between devices with their start and end apart: 36, of which 13 were waited for; matrix products, arithmetic and copies ran while one was open for 0% of the time, Pallas kernels for 18%

profile of v2, /device:TPU:8, one launch (start us, length us, event | category | flops | bytes accessed | tf_op | source)
XLA Modules:
  0.0 106.3 jit_solution(76094929840068758)
XLA Ops:
  0.6 6.4 %collective-permute-start.2 = (bf16[16,2304]{1,0:T(8,128)(2,1)}, bf16[16,2304]{1,0:T(8,128)(2,1)S(1)}, u32[]{:S(2)}, u32[]{:S(2)}) collective-permute-start(bf16[16,2304]{1,0:T(8,128)(2,1)} %bitcast.10), channel_id=1, source_target_pairs={{0,6},{2,0},{4,2},{6,4},{1,7},{3,1},{5,3},{7,5},{8,14},{10,8},{12,... | collective-permute-start | bytes 221192 | tf_op jit(solution)/shard_map/ppermute | solution.py:232
  7.0 3.8 %collective-permute-start = (bf16[16,2304]{1,0:T(8,128)(2,1)}, bf16[16,2304]{1,0:T(8,128)(2,1)S(1)}, u32[]{:S(2)}, u32[]{:S(2)}) collective-permute-start(bf16[16,2304]{1,0:T(8,128)(2,1)} %bitcast.12), channel_id=1, source_target_pairs={{0,4},{2,6},{4,0},{6,2},{1,5},{3,7},{5,1},{7,3},{8,12},{10,14},{12... | collective-permute-start | bytes 221192 | tf_op jit(solution)/shard_map/ppermute | solution.py:232
  11.6 3.5 %dequant.2.w_ref = bf16[2304,1280]{1,0:T(8,128)(2,1)S(1)} custom-call(f32[10,1,18]{2,1,0:T(1,128)S(1)} %bitcast.14, bf16[2304,1280]{1,0:T(8,128)(2,1)} %bitcast.16), custom_call_target="tpu_custom_call" | custom-call | flops 2949120 | bytes 11796480 | tf_op jit(solution)/shard_map/dequant/pallas_call | solution.py:72
  18.0 2.7 %collective-permute-start.4 = (bf16[32,2304]{1,0:T(8,128)(2,1)S(1)}, bf16[32,2304]{1,0:T(8,128)(2,1)S(1)}, u32[]{:S(2)}, u32[]{:S(2)}) collective-permute-start(bf16[32,2304]{1,0:T(8,128)(2,1)S(1)} %join.4.refs_0_), channel_id=1, source_target_pairs={{0,16},{8,24},{16,0},{24,8},{1,17},{9,25},{17,1},{25,9},{2,18},{10... | collective-permute-start | bytes 442376 | tf_op jit(solution)/shard_map/ppermute | solution.py:232
  23.9 3.0 %collective-permute-done.4.refs_2_ = bf16[32,2304]{1,0:T(8,128)(2,1)S(1)} collective-permute-done((bf16[32,2304]{1,0:T(8,128)(2,1)S(1)}, bf16[32,2304]{1,0:T(8,128)(2,1)S(1)}, u32[]{:S(2)}, u32[]{:S(2)}) %collective-permute-start.4) | collective-permute-done | bytes 147488 | tf_op jit(solution)/shard_map/ppermute | solution.py:232
  27.1 2.6 %collective-permute-start.20 = (bf16[32,2304]{1,0:T(8,128)(2,1)S(1)}, bf16[32,2304]{1,0:T(8,128)(2,1)S(1)}, u32[]{:S(2)}, u32[]{:S(2)}) collective-permute-start(bf16[32,2304]{1,0:T(8,128)(2,1)S(1)} %join.6.refs_0_), channel_id=1, source_target_pairs={{0,24},{8,0},{16,8},{24,16},{1,25},{9,1},{17,9},{25,17},{2,26},{10... | collective-permute-start | bytes 442376 | tf_op jit(solution)/shard_map/ppermute | solution.py:232
  29.7 2.2 %collective-permute-start.21 = (bf16[32,2304]{1,0:T(8,128)(2,1)S(1)}, bf16[32,2304]{1,0:T(8,128)(2,1)S(1)}, u32[]{:S(2)}, u32[]{:S(2)}) collective-permute-start(bf16[32,2304]{1,0:T(8,128)(2,1)S(1)} %join.6.refs_0_), channel_id=1, source_target_pairs={{0,16},{8,24},{16,0},{24,8},{1,17},{9,25},{17,1},{25,9},{2,18},{10... | collective-permute-start | bytes 442376 | tf_op jit(solution)/shard_map/ppermute | solution.py:232
  31.8 2.3 %encode.2 = (bf16[64,1280]{1,0:T(8,128)(2,1)S(1)}, bf16[64,1280]{1,0:T(8,128)(2,1)S(1)}, bf16[64,1280]{1,0:T(8,128)(2,1)S(1)}, bf16[64,1280]{1,0:T(8,128)(2,1)S(1)}) custom-call(s32[4]{0:T(128)S(1)} %pad_add_fusion.where_ref, bf16[128,2304]{1,0:T(8,128)(2,1)S(1)} %join.5.mine_ref, bf16[128,2304]{1,0:T(8,128)(2,1)S(1)} %collective-permute-done.6.theirs_ref, ...), custom_call_target="tpu_custom_call" | custom-call | flops 1509949440 | bytes 5898240 | tf_op jit(solution)/shard_map/encode/pallas_call | solution.py:109
  34.1 3.5 %dequant.3.refs_4_ = bf16[1280,2304]{1,0:T(8,128)(2,1)S(1)} custom-call(f32[10,1,18]{2,1,0:T(1,128)S(1)} %bitcast.15, bf16[1280,2304]{1,0:T(8,128)(2,1)} %bitcast.17), custom_call_target="tpu_custom_call" | custom-call | flops 2949120 | bytes 11796480 | tf_op jit(solution)/shard_map/dequant/pallas_call | solution.py:72
  37.7 2.3 %collective-permute-done.22.refs_3_ = bf16[32,2304]{1,0:T(8,128)(2,1)S(1)} collective-permute-done((bf16[32,2304]{1,0:T(8,128)(2,1)S(1)}, bf16[32,2304]{1,0:T(8,128)(2,1)S(1)}, u32[]{:S(2)}, u32[]{:S(2)}) %collective-permute-start.22) | collective-permute-done | bytes 147488 | tf_op jit(solution)/shard_map/ppermute | solution.py:232
  42.3 2.3 %collective-permute-start.9 = (bf16[64,1280]{1,0:T(8,128)(2,1)S(1)}, bf16[64,1280]{1,0:T(8,128)(2,1)S(1)}, u32[]{:S(2)}, u32[]{:S(2)}) collective-permute-start(bf16[64,1280]{1,0:T(8,128)(2,1)S(1)} %get-tuple-element.40), channel_id=1, source_target_pairs={{0,128},{64,192},{128,0},{192,64},{1,129},{65,193},{129,1},{193,65... | collective-permute-start | bytes 491528 | tf_op jit(solution)/shard_map/ppermute | solution.py:232
  44.6 2.3 %encode.3 = (bf16[64,1280]{1,0:T(8,128)(2,1)S(1)}, bf16[64,1280]{1,0:T(8,128)(2,1)S(1)}, bf16[64,1280]{1,0:T(8,128)(2,1)S(1)}, bf16[64,1280]{1,0:T(8,128)(2,1)S(1)}) custom-call(s32[4]{0:T(128)S(1)} %pad_add_fusion.where_ref, bf16[128,2304]{1,0:T(8,128)(2,1)S(1)} %join.7.mine_ref, bf16[128,2304]{1,0:T(8,128)(2,1)S(1)} %collective-permute-done.23.theirs_ref, ...), custom_call_target="tpu_custom_call" | custom-call | flops 1509949440 | bytes 5898240 | tf_op jit(solution)/shard_map/encode/pallas_call | solution.py:109
  50.3 2.8 %collective-permute-done.9.refs_3_ = bf16[64,1280]{1,0:T(8,128)(2,1)S(1)} collective-permute-done((bf16[64,1280]{1,0:T(8,128)(2,1)S(1)}, bf16[64,1280]{1,0:T(8,128)(2,1)S(1)}, u32[]{:S(2)}, u32[]{:S(2)}) %collective-permute-start.9) | collective-permute-done | bytes 163872 | tf_op jit(solution)/shard_map/ppermute | solution.py:232
  56.5 2.8 %collective-permute-done.26.refs_3_ = bf16[64,1280]{1,0:T(8,128)(2,1)S(1)} collective-permute-done((bf16[64,1280]{1,0:T(8,128)(2,1)S(1)}, bf16[64,1280]{1,0:T(8,128)(2,1)S(1)}, u32[]{:S(2)}, u32[]{:S(2)}) %collective-permute-start.26) | collective-permute-done | bytes 163872 | tf_op jit(solution)/shard_map/ppermute | solution.py:232
  61.2 2.9 %collective-permute-start.12 = (bf16[64,1280]{1,0:T(8,128)(2,1)S(1)}, bf16[64,1280]{1,0:T(8,128)(2,1)S(1)}, u32[]{:S(2)}, u32[]{:S(2)}) collective-permute-start(bf16[64,1280]{1,0:T(8,128)(2,1)S(1)} %activate.2.refs_0_), channel_id=1, source_target_pairs={{0,128},{64,192},{128,0},{192,64},{1,129},{65,193},{129,1},{193,65... | collective-permute-start | bytes 491528 | tf_op jit(solution)/shard_map/ppermute | solution.py:232
  66.3 2.1 %collective-permute-start.29 = (bf16[64,1280]{1,0:T(8,128)(2,1)S(1)}, bf16[64,1280]{1,0:T(8,128)(2,1)S(1)}, u32[]{:S(2)}, u32[]{:S(2)}) collective-permute-start(bf16[64,1280]{1,0:T(8,128)(2,1)S(1)} %activate.3.refs_0_.refs_4_), channel_id=1, source_target_pairs={{0,128},{64,192},{128,0},{192,64},{1,129},{65,193},{129,1},{193,65... | collective-permute-start | bytes 491528 | tf_op jit(solution)/shard_map/ppermute | solution.py:232
  68.3 4.6 %collective-permute-start.28 = (bf16[64,1280]{1,0:T(8,128)(2,1)S(1)}, bf16[64,1280]{1,0:T(8,128)(2,1)S(1)}, u32[]{:S(2)}, u32[]{:S(2)}) collective-permute-start(bf16[64,1280]{1,0:T(8,128)(2,1)S(1)} %activate.3.refs_0_.refs_4_), channel_id=1, source_target_pairs={{0,192},{64,0},{128,64},{192,128},{1,193},{65,1},{129,65},{193,129... | collective-permute-start | bytes 491528 | tf_op jit(solution)/shard_map/ppermute | solution.py:232
  74.8 2.3 %decode.2 = (bf16[128,2304]{1,0:T(8,128)(2,1)S(1)}, bf16[128,2304]{1,0:T(8,128)(2,1)S(1)}) custom-call(s32[4]{0:T(128)S(1)} %pad_add_fusion.where_ref, bf16[64,1280]{1,0:T(8,128)(2,1)S(1)} %activate.2.refs_0_, bf16[64,1280]{1,0:T(8,128)(2,1)S(1)} %collective-permute-done.11.refs_1_, bf16[64,1280]{1,0:T(8,128)(2,1)S(1)} %collective-permute-done.12.refs_2_, ...), custom_call_target="tpu_custom_call" | custom-call | flops 1509949440 | bytes 5898240 | tf_op jit(solution)/shard_map/decode/pallas_call | solution.py:139
  78.5 2.3 %decode.3 = (bf16[128,2304]{1,0:T(8,128)(2,1)S(1)}, bf16[128,2304]{1,0:T(8,128)(2,1)S(1)}) custom-call(s32[4]{0:T(128)S(1)} %pad_add_fusion.where_ref, bf16[64,1280]{1,0:T(8,128)(2,1)S(1)} %activate.3.refs_0_.refs_4_, bf16[64,1280]{1,0:T(8,128)(2,1)S(1)} %collective-permute-done.28.refs_1_.refs_5_, ...), custom_call_target="tpu_custom_call" | custom-call | flops 1509949440 | bytes 5898240 | tf_op jit(solution)/shard_map/decode/pallas_call | solution.py:139
  81.1 3.2 %collective-permute-start.16 = (bf16[32,2304]{1,0:T(8,128)(2,1)S(1)}, bf16[32,2304]{1,0:T(8,128)(2,1)S(1)}, u32[]{:S(2)}, u32[]{:S(2)}) collective-permute-start(bf16[32,2304]{1,0:T(8,128)(2,1)S(1)} %get-tuple-element.45), channel_id=1, source_target_pairs={{0,24},{8,0},{16,8},{24,16},{1,25},{9,1},{17,9},{25,17},{2,26},{10... | collective-permute-start | bytes 442376 | tf_op jit(solution)/shard_map/ppermute | solution.py:232
  85.4 2.4 %collective-permute-start.33 = (bf16[32,2304]{1,0:T(8,128)(2,1)S(1)}, bf16[32,2304]{1,0:T(8,128)(2,1)S(1)}, u32[]{:S(2)}, u32[]{:S(2)}) collective-permute-start(bf16[32,2304]{1,0:T(8,128)(2,1)S(1)} %get-tuple-element.60), channel_id=1, source_target_pairs={{0,24},{8,0},{16,8},{24,16},{1,25},{9,1},{17,9},{25,17},{2,26},{10... | collective-permute-start | bytes 442376 | tf_op jit(solution)/shard_map/ppermute | solution.py:232
  87.8 3.4 %collective-permute-done.15.refs_1_ = bf16[32,2304]{1,0:T(8,128)(2,1)S(1)} collective-permute-done((bf16[32,2304]{1,0:T(8,128)(2,1)S(1)}, bf16[32,2304]{1,0:T(8,128)(2,1)S(1)}, u32[]{:S(2)}, u32[]{:S(2)}) %collective-permute-start.15) | collective-permute-done | bytes 147488 | tf_op jit(solution)/shard_map/ppermute | solution.py:232
  94.4 3.7 %collective-permute-start.19 = (bf16[16,2304]{1,0:T(8,128)(2,1)S(1)}, bf16[16,2304]{1,0:T(8,128)(2,1)S(1)}, u32[]{:S(2)}, u32[]{:S(2)}) collective-permute-start(bf16[16,2304]{1,0:T(8,128)(2,1)S(1)} %get-tuple-element.48), channel_id=1, source_target_pairs={{0,6},{2,0},{4,2},{6,4},{1,7},{3,1},{5,3},{7,5},{8,14},{10,8},{12,... | collective-permute-start | bytes 221192 | tf_op jit(solution)/shard_map/ppermute | solution.py:232
  101.9 3.7 %collective-permute-done.35.refs_3_ = bf16[16,2304]{1,0:T(8,128)(2,1)S(1)} collective-permute-done((bf16[16,2304]{1,0:T(8,128)(2,1)S(1)}, bf16[16,2304]{1,0:T(8,128)(2,1)S(1)}, u32[]{:S(2)}, u32[]{:S(2)}) %collective-permute-start.35) | collective-permute-done | bytes 73760 | tf_op jit(solution)/shard_map/ppermute | solution.py:232
  (79 shorter events, 32.4 us)
Async XLA Ops:
  0.6 14.5 %collective-permute-start.2 = (bf16[16,2304]{1,0:T(8,128)(2,1)}, bf16[16,2304]{1,0:T(8,128)(2,1)S(1)}, u32[]{:S(2)}, u32[]{:S(2)}) collective-permute-start(bf16[16,2304]{1,0:T(8,128)(2,1)} %bitcast.10), channel_id=1, source_target_pairs={{0,6},{2,0},{4,2},{6,4},{1,7},{3,1},{5,3},{7,5},{8,14},{10,8},{12,... | collective-permute-start | bytes 221192 | tf_op jit(solution)/shard_map/ppermute | solution.py:232
  7.0 9.4 %collective-permute-start.1 = (bf16[16,2304]{1,0:T(8,128)(2,1)}, bf16[16,2304]{1,0:T(8,128)(2,1)S(1)}, u32[]{:S(2)}, u32[]{:S(2)}) collective-permute-start(bf16[16,2304]{1,0:T(8,128)(2,1)} %bitcast.11), channel_id=1, source_target_pairs={{0,2},{2,4},{4,6},{6,0},{1,3},{3,5},{5,7},{7,1},{8,10},{10,12},{12... | collective-permute-start | bytes 221192 | tf_op jit(solution)/shard_map/ppermute | solution.py:232
  7.0 9.4 %collective-permute-start = (bf16[16,2304]{1,0:T(8,128)(2,1)}, bf16[16,2304]{1,0:T(8,128)(2,1)S(1)}, u32[]{:S(2)}, u32[]{:S(2)}) collective-permute-start(bf16[16,2304]{1,0:T(8,128)(2,1)} %bitcast.12), channel_id=1, source_target_pairs={{0,4},{2,6},{4,0},{6,2},{1,5},{3,7},{5,1},{7,3},{8,12},{10,14},{12... | collective-permute-start | bytes 221192 | tf_op jit(solution)/shard_map/ppermute | solution.py:232
  18.0 8.8 %collective-permute-start.4 = (bf16[32,2304]{1,0:T(8,128)(2,1)S(1)}, bf16[32,2304]{1,0:T(8,128)(2,1)S(1)}, u32[]{:S(2)}, u32[]{:S(2)}) collective-permute-start(bf16[32,2304]{1,0:T(8,128)(2,1)S(1)} %join.4.refs_0_), channel_id=1, source_target_pairs={{0,16},{8,24},{16,0},{24,8},{1,17},{9,25},{17,1},{25,9},{2,18},{10... | collective-permute-start | bytes 442376 | tf_op jit(solution)/shard_map/ppermute | solution.py:232
  27.1 10.6 %collective-permute-start.20 = (bf16[32,2304]{1,0:T(8,128)(2,1)S(1)}, bf16[32,2304]{1,0:T(8,128)(2,1)S(1)}, u32[]{:S(2)}, u32[]{:S(2)}) collective-permute-start(bf16[32,2304]{1,0:T(8,128)(2,1)S(1)} %join.6.refs_0_), channel_id=1, source_target_pairs={{0,24},{8,0},{16,8},{24,16},{1,25},{9,1},{17,9},{25,17},{2,26},{10... | collective-permute-start | bytes 442376 | tf_op jit(solution)/shard_map/ppermute | solution.py:232
  29.7 10.3 %collective-permute-start.22 = (bf16[32,2304]{1,0:T(8,128)(2,1)S(1)}, bf16[32,2304]{1,0:T(8,128)(2,1)S(1)}, u32[]{:S(2)}, u32[]{:S(2)}) collective-permute-start(bf16[32,2304]{1,0:T(8,128)(2,1)S(1)} %join.6.refs_0_), channel_id=1, source_target_pairs={{0,8},{8,16},{16,24},{24,0},{1,9},{9,17},{17,25},{25,1},{2,10},{10... | collective-permute-start | bytes 442376 | tf_op jit(solution)/shard_map/ppermute | solution.py:232
  29.7 10.3 %collective-permute-start.21 = (bf16[32,2304]{1,0:T(8,128)(2,1)S(1)}, bf16[32,2304]{1,0:T(8,128)(2,1)S(1)}, u32[]{:S(2)}, u32[]{:S(2)}) collective-permute-start(bf16[32,2304]{1,0:T(8,128)(2,1)S(1)} %join.6.refs_0_), channel_id=1, source_target_pairs={{0,16},{8,24},{16,0},{24,8},{1,17},{9,25},{17,1},{25,9},{2,18},{10... | collective-permute-start | bytes 442376 | tf_op jit(solution)/shard_map/ppermute | solution.py:232
  40.1 8.8 %collective-permute-start.7 = (bf16[64,1280]{1,0:T(8,128)(2,1)S(1)}, bf16[64,1280]{1,0:T(8,128)(2,1)S(1)}, u32[]{:S(2)}, u32[]{:S(2)}) collective-permute-start(bf16[64,1280]{1,0:T(8,128)(2,1)S(1)} %get-tuple-element.38), channel_id=1, source_target_pairs={{0,64},{64,128},{128,192},{192,0},{1,65},{65,129},{129,193},{193,1... | collective-permute-start | bytes 491528 | tf_op jit(solution)/shard_map/ppermute | solution.py:232
  41.8 8.5 %collective-permute-start.8 = (bf16[64,1280]{1,0:T(8,128)(2,1)S(1)}, bf16[64,1280]{1,0:T(8,128)(2,1)S(1)}, u32[]{:S(2)}, u32[]{:S(2)}) collective-permute-start(bf16[64,1280]{1,0:T(8,128)(2,1)S(1)} %get-tuple-element.39), channel_id=1, source_target_pairs={{0,192},{64,0},{128,64},{192,128},{1,193},{65,1},{129,65},{193,129... | collective-permute-start | bytes 491528 | tf_op jit(solution)/shard_map/ppermute | solution.py:232
  42.3 10.9 %collective-permute-start.9 = (bf16[64,1280]{1,0:T(8,128)(2,1)S(1)}, bf16[64,1280]{1,0:T(8,128)(2,1)S(1)}, u32[]{:S(2)}, u32[]{:S(2)}) collective-permute-start(bf16[64,1280]{1,0:T(8,128)(2,1)S(1)} %get-tuple-element.40), channel_id=1, source_target_pairs={{0,128},{64,192},{128,0},{192,64},{1,129},{65,193},{129,1},{193,65... | collective-permute-start | bytes 491528 | tf_op jit(solution)/shard_map/ppermute | solution.py:232
  46.8 8.0 %collective-permute-start.24 = (bf16[64,1280]{1,0:T(8,128)(2,1)S(1)}, bf16[64,1280]{1,0:T(8,128)(2,1)S(1)}, u32[]{:S(2)}, u32[]{:S(2)}) collective-permute-start(bf16[64,1280]{1,0:T(8,128)(2,1)S(1)} %get-tuple-element.52), channel_id=1, source_target_pairs={{0,64},{64,128},{128,192},{192,0},{1,65},{65,129},{129,193},{193,1... | collective-permute-start | bytes 491528 | tf_op jit(solution)/shard_map/ppermute | solution.py:232
  47.7 8.8 %collective-permute-start.25 = (bf16[64,1280]{1,0:T(8,128)(2,1)S(1)}, bf16[64,1280]{1,0:T(8,128)(2,1)S(1)}, u32[]{:S(2)}, u32[]{:S(2)}) collective-permute-start(bf16[64,1280]{1,0:T(8,128)(2,1)S(1)} %get-tuple-element.53), channel_id=1, source_target_pairs={{0,192},{64,0},{128,64},{192,128},{1,193},{65,1},{129,65},{193,129... | collective-permute-start | bytes 491528 | tf_op jit(solution)/shard_map/ppermute | solution.py:232
  48.9 10.4 %collective-permute-start.26 = (bf16[64,1280]{1,0:T(8,128)(2,1)S(1)}, bf16[64,1280]{1,0:T(8,128)(2,1)S(1)}, u32[]{:S(2)}, u32[]{:S(2)}) collective-permute-start(bf16[64,1280]{1,0:T(8,128)(2,1)S(1)} %get-tuple-element.54), channel_id=1, source_target_pairs={{0,128},{64,192},{128,0},{192,64},{1,129},{65,193},{129,1},{193,65... | collective-permute-start | bytes 491528 | tf_op jit(solution)/shard_map/ppermute | solution.py:232
  61.2 11.7 %collective-permute-start.12 = (bf16[64,1280]{1,0:T(8,128)(2,1)S(1)}, bf16[64,1280]{1,0:T(8,128)(2,1)S(1)}, u32[]{:S(2)}, u32[]{:S(2)}) collective-permute-start(bf16[64,1280]{1,0:T(8,128)(2,1)S(1)} %activate.2.refs_0_), channel_id=1, source_target_pairs={{0,128},{64,192},{128,0},{192,64},{1,129},{65,193},{129,1},{193,65... | collective-permute-start | bytes 491528 | tf_op jit(solution)/shard_map/ppermute | solution.py:232
  64.1 10.7 %collective-permute-start.11 = (bf16[64,1280]{1,0:T(8,128)(2,1)S(1)}, bf16[64,1280]{1,0:T(8,128)(2,1)S(1)}, u32[]{:S(2)}, u32[]{:S(2)}) collective-permute-start(bf16[64,1280]{1,0:T(8,128)(2,1)S(1)} %activate.2.refs_0_), channel_id=1, source_target_pairs={{0,192},{64,0},{128,64},{192,128},{1,193},{65,1},{129,65},{193,129... | collective-permute-start | bytes 491528 | tf_op jit(solution)/shard_map/ppermute | solution.py:232
  65.5 12.0 %collective-permute-start.30 = (bf16[64,1280]{1,0:T(8,128)(2,1)S(1)}, bf16[64,1280]{1,0:T(8,128)(2,1)S(1)}, u32[]{:S(2)}, u32[]{:S(2)}) collective-permute-start(bf16[64,1280]{1,0:T(8,128)(2,1)S(1)} %activate.3.refs_0_.refs_4_), channel_id=1, source_target_pairs={{0,64},{64,128},{128,192},{192,0},{1,65},{65,129},{129,193},{193,1... | collective-permute-start | bytes 491528 | tf_op jit(solution)/shard_map/ppermute | solution.py:232
  66.3 11.2 %collective-permute-start.29 = (bf16[64,1280]{1,0:T(8,128)(2,1)S(1)}, bf16[64,1280]{1,0:T(8,128)(2,1)S(1)}, u32[]{:S(2)}, u32[]{:S(2)}) collective-permute-start(bf16[64,1280]{1,0:T(8,128)(2,1)S(1)} %activate.3.refs_0_.refs_4_), channel_id=1, source_target_pairs={{0,128},{64,192},{128,0},{192,64},{1,129},{65,193},{129,1},{193,65... | collective-permute-start | bytes 491528 | tf_op jit(solution)/shard_map/ppermute | solution.py:232
  68.3 10.1 %collective-permute-start.28 = (bf16[64,1280]{1,0:T(8,128)(2,1)S(1)}, bf16[64,1280]{1,0:T(8,128)(2,1)S(1)}, u32[]{:S(2)}, u32[]{:S(2)}) collective-permute-start(bf16[64,1280]{1,0:T(8,128)(2,1)S(1)} %activate.3.refs_0_.refs_4_), channel_id=1, source_target_pairs={{0,192},{64,0},{128,64},{192,128},{1,193},{65,1},{129,65},{193,129... | collective-permute-start | bytes 491528 | tf_op jit(solution)/shard_map/ppermute | solution.py:232
  81.0 10.2 %collective-permute-start.15 = (bf16[32,2304]{1,0:T(8,128)(2,1)S(1)}, bf16[32,2304]{1,0:T(8,128)(2,1)S(1)}, u32[]{:S(2)}, u32[]{:S(2)}) collective-permute-start(bf16[32,2304]{1,0:T(8,128)(2,1)S(1)} %get-tuple-element.44), channel_id=1, source_target_pairs={{0,8},{8,16},{16,24},{24,0},{1,9},{9,17},{17,25},{25,1},{2,10},{10... | collective-permute-start | bytes 442376 | tf_op jit(solution)/shard_map/ppermute | solution.py:232
  81.1 10.6 %collective-permute-start.16 = (bf16[32,2304]{1,0:T(8,128)(2,1)S(1)}, bf16[32,2304]{1,0:T(8,128)(2,1)S(1)}, u32[]{:S(2)}, u32[]{:S(2)}) collective-permute-start(bf16[32,2304]{1,0:T(8,128)(2,1)S(1)} %get-tuple-element.45), channel_id=1, source_target_pairs={{0,24},{8,0},{16,8},{24,16},{1,25},{9,1},{17,9},{25,17},{2,26},{10... | collective-permute-start | bytes 442376 | tf_op jit(solution)/shard_map/ppermute | solution.py:232
  84.3 8.2 %collective-permute-start.17 = (bf16[32,2304]{1,0:T(8,128)(2,1)S(1)}, bf16[32,2304]{1,0:T(8,128)(2,1)S(1)}, u32[]{:S(2)}, u32[]{:S(2)}) collective-permute-start(bf16[32,2304]{1,0:T(8,128)(2,1)S(1)} %get-tuple-element.46), channel_id=1, source_target_pairs={{0,16},{8,24},{16,0},{24,8},{1,17},{9,25},{17,1},{25,9},{2,18},{10... | collective-permute-start | bytes 442376 | tf_op jit(solution)/shard_map/ppermute | solution.py:232
  84.5 13.5 %collective-permute-start.32 = (bf16[32,2304]{1,0:T(8,128)(2,1)S(1)}, bf16[32,2304]{1,0:T(8,128)(2,1)S(1)}, u32[]{:S(2)}, u32[]{:S(2)}) collective-permute-start(bf16[32,2304]{1,0:T(8,128)(2,1)S(1)} %get-tuple-element.59), channel_id=1, source_target_pairs={{0,8},{8,16},{16,24},{24,0},{1,9},{9,17},{17,25},{25,1},{2,10},{10... | collective-permute-start | bytes 442376 | tf_op jit(solution)/shard_map/ppermute | solution.py:232
  85.4 12.6 %collective-permute-start.33 = (bf16[32,2304]{1,0:T(8,128)(2,1)S(1)}, bf16[32,2304]{1,0:T(8,128)(2,1)S(1)}, u32[]{:S(2)}, u32[]{:S(2)}) collective-permute-start(bf16[32,2304]{1,0:T(8,128)(2,1)S(1)} %get-tuple-element.60), channel_id=1, source_target_pairs={{0,24},{8,0},{16,8},{24,16},{1,25},{9,1},{17,9},{25,17},{2,26},{10... | collective-permute-start | bytes 442376 | tf_op jit(solution)/shard_map/ppermute | solution.py:232
  92.7 9.2 %collective-permute-start.18 = (bf16[16,2304]{1,0:T(8,128)(2,1)S(1)}, bf16[16,2304]{1,0:T(8,128)(2,1)S(1)}, u32[]{:S(2)}, u32[]{:S(2)}) collective-permute-start(bf16[16,2304]{1,0:T(8,128)(2,1)S(1)} %get-tuple-element.47), channel_id=1, source_target_pairs={{0,4},{2,6},{4,0},{6,2},{1,5},{3,7},{5,1},{7,3},{8,12},{10,14},{12... | collective-permute-start | bytes 221192 | tf_op jit(solution)/shard_map/ppermute | solution.py:232
  (17 other events, 159.9 us)

commit v3 on v2

--- a/solution.py
+++ b/solution.py
@@ -10,7 +10,8 @@
 BLOCK = 128
 Y, ZL, X, ZH, C = 4, 2, 4, 4, 2
 LAYER, LAT = ("y", "zl"), ("x", "zh", "c")
-AROUND = (1, 3, 2)
+ORDER = (0, 2, 1, 3)
+SENT = (2, 3, 1)
 F32, BF16 = jnp.float32, jnp.bfloat16
 MIB = 1 << 20
 IN_VMEM = pl.BlockSpec(memory_space=pltpu.VMEM)
@@ -88,42 +89,43 @@
         store(at, jnp.dot(rows, w_ref[:, at], preferred_element_type=F32).astype(BF16))
 
 
-def encode_kernel(where_ref, mine_ref, theirs_ref, w_ref, *refs):
-    outs, all_ref = refs[:Y], refs[Y]
+def encode_kernel(where_ref, *refs, pieces, chunk):
+    w_ref, outs, all_ref = refs[pieces], refs[pieces + 1 : pieces + 1 + Y], refs[-1]
     height = outs[0].shape[0]
+    count = height * Y // pieces
     y = where_ref[0]
-    rows = jnp.concatenate([mine_ref[...], theirs_ref[...]], axis=0)
+    rows = jnp.concatenate([ref[chunk * count : (chunk + 1) * count, :] for ref in refs[:pieces]], axis=0)
 
     def store(at, tile):
         all_ref[:, at] = tile
 
     product(rows, w_ref, store)
-    for r, out in enumerate(outs):
-        quarter = lax.rem(y + r, Y)
+    for p, out in enumerate(outs):
+        quarter = lax.rem(y + ORDER[p], Y)
         out[...] = all_ref[pl.ds(pl.multiple_of(quarter * height, height), height), :]
 
 
-def encode(where, mine, theirs, weight):
+def encode(where, pieces, weight, chunk, chunks):
     depth, width = weight.shape
-    rows = mine.shape[0] + theirs.shape[0]
-    return pl.pallas_call(
-        encode_kernel,
-        in_specs=[IN_SMEM] + [IN_VMEM] * 3,
+    rows = sum(piece.shape[0] for piece in pieces) // chunks
+    return pl.pallas_call(
+        functools.partial(encode_kernel, pieces=len(pieces), chunk=chunk),
+        in_specs=[IN_SMEM] + [IN_VMEM] * (len(pieces) + 1),
         out_specs=[IN_VMEM] * Y,
         out_shape=[shape(rows // Y, width)] * Y,
         scratch_shapes=[pltpu.VMEM((rows, width), BF16)],
         compiler_params=params(16),
         cost_estimate=cost(2 * rows * depth * width, 2 * depth * width),
         name="encode",
-    )(where, mine, theirs, weight)
+    )(where, *pieces, weight)
 
 
 def decode_kernel(where_ref, *refs):
     quarters, w_ref, mine_ref, theirs_ref, all_ref = refs[:Y], refs[Y], refs[Y + 1], refs[Y + 2], refs[Y + 3]
     height, half = quarters[0].shape[0], mine_ref.shape[0]
     y = where_ref[0]
-    for r, ref in enumerate(quarters):
-        quarter = lax.rem(y + r, Y)
+    for p, ref in enumerate(quarters):
+        quarter = lax.rem(y + ORDER[p], Y)
         all_ref[pl.ds(pl.multiple_of(quarter * height, height), height), :] = ref[...]
 
     def store(at, tile):
@@ -191,10 +193,11 @@
     blocks = latents[0].shape[0] // height
     copies = []
     for a, ref in enumerate(latents):
-        n, quarter = a // Y, lax.rem(y + a % Y, Y)
+        n, quarter = a // Y, lax.rem(y + ORDER[a % Y], Y)
         for j in range(blocks):
             b = quarter * blocks + j
-            kc, kx, k = b // (2 * X), lax.rem(b // 2, X), lax.rem(b, 2)
+            kc, p, k = b // (2 * X), lax.rem(b // 2, X), lax.rem(b, 2)
+            kx = jnp.where(p == 1, ORDER[1], jnp.where(p == 2, ORDER[2], p))
             owner = (lax.rem(x + kx, X) * ZH + lax.rem(zh + 2 * (1 - n) + k, ZH)) * C + lax.rem(c + kc, C)
             copies.append(
                 pltpu.make_async_copy(
@@ -233,12 +236,11 @@
 
 
 def fetch_around(array, axis, size):
-    got = {k: send(array, axis, size, -k) for k in AROUND}
-    return [array] + [got[k] for k in (1, 2, 3)]
+    return [array] + [send(array, axis, size, -k) for k in ORDER[1:]]
 
 
 def hand_around(arrays, axis, size):
-    return [arrays[0]] + [send(arrays[k], axis, size, k) for k in AROUND]
+    return [arrays[0]] + [send(arrays[p], axis, size, ORDER[p]) for p in SENT]
 
 
 def on_device(acts, enc_weight, enc_scale, enc_bias, dec_weight, dec_scale, dec_bias):
@@ -249,33 +251,34 @@
     where = jnp.stack([lax.axis_index(a) for a in ("y", "x", "zh", "c")]).astype(jnp.int32)
     near, far, back = (send(own, "zh", ZH, -k) for k in (1, 2, 3))
     enc_full = dequant(enc_weight[0], after(jnp.transpose(enc_scale, (2, 0, 1)), where), 2 * BLOCK, False)
-    pairs = ([far, after(back, enc_full, near)], [own, near])
-    quarters, pieces, terms = [], None, None
-    for n, pair in enumerate(pairs):
-        if n == 1:
-            pair[1] = after(pair[1], pieces[1])
-        column = whole(join_kernel, pair, [shape(chunk, depth)], "join")[0]
-        pieces = fetch_around(column, "x", X)
-        if n == 1:
-            pieces[1] = after(pieces[1], terms[0])
-        mine = whole(join_kernel, pieces, [shape(X * chunk, depth)], "join")[0]
-        theirs = send(mine, "c", C, 1)
-        terms = list(encode(where, mine, theirs, enc_full))
-        if n == 0:
-            dec_full = dequant(dec_weight[0], after(jnp.transpose(dec_scale, (1, 0, 2)), terms[0]), BLOCK, True)
-            terms[0] = after(terms[0], dec_full)
-        part = added(hand_around(terms, "y", Y), 1, "gather")[0]
-        latents = whole(activate_kernel, [part, send(part, "zl", ZL, 1), enc_bias], [shape(*part.shape)], "activate")[0]
+    column = whole(join_kernel, [far, back, own, after(near, enc_full)], [shape(ZH * rows, depth)], "join")[0]
+    dec_full = dequant(dec_weight[0], after(jnp.transpose(dec_scale, (1, 0, 2)), column), BLOCK, True)
+    mine = fetch_around(column, "x", X)
+    theirs = [send(piece, "c", C, 1) for piece in mine[:1] + [after(piece, dec_full) for piece in mine[1:]]]
+    pieces = mine + theirs
+    quarters, own_piece = [], pieces[0]
+    for n in range(2):
+        terms = list(encode(where, [own_piece] + pieces[1:], enc_full, n, 2))
+        own_piece = after(own_piece, terms[0])
+        got = hand_around(terms, "y", Y)
+        part = added(got, 1, "gather")[0]
+        other = send(part, "zl", ZL, 1)
+        if False and n == 1:
+            other = after(other, quarters[0][1])
+        latents = whole(activate_kernel, [part, other, enc_bias], [shape(*part.shape)], "activate")[0]
         quarters.append(fetch_around(latents, "y", Y))
-    parts, done = [], None
+    parts, decoded, got = [], None, None
     for n in range(2):
-        latents = list(quarters[n])
-        if done is not None:
-            latents[0] = after(latents[0], done)
-        mine, theirs = decode(where, latents, dec_full)
-        done = mine
-        cuts = added([mine, send(theirs, "c", C, 1)], X, "add")
-        low, high = added(hand_around(cuts, "x", X), 2, "fold")
+        own_part = quarters[n][0] if n == 0 else after(quarters[n][0], decoded)
+        decoded, theirs = decode(where, [own_part] + quarters[n][1:], dec_full)
+        theirs = send(theirs, "c", C, 1)
+        if True and n == 1:
+            theirs = after(theirs, got[1])
+        cuts = added([decoded, theirs], X, "add")
+        got = hand_around(cuts, "x", X)
+        if False and n == 1:
+            got[0] = after(got[0], parts[1])
+        low, high = added(got, 2, "fold")
         parts += [send(low, "zh", ZH, 2), send(high, "zh", ZH, 3)] if n == 0 else [low, send(high, "zh", ZH, 1)]
     recon = whole(finish_kernel, parts + [dec_bias], [shape(rows, depth)], "finish")[0]
     return (recon[None], place(where, quarters[0] + quarters[1]))

time: 108 us -> 104 us (0.963)
  starting transfers between devices: 57.9 us -> 47.8 us
  waiting for transfers between devices: 27.1 us -> 33.1 us
    ppermute x36 -> x35, starting transfers between devices: 57.9 us -> 47.8 us  [send(): lax.ppermute(array, axis, [(i, (i + by) % size) for i in range(size)])]
    ppermute x36 -> x35, waiting for transfers between devices: 27.1 us -> 33.1 us  [send(): lax.ppermute(array, axis, [(i, (i + by) % size) for i in range(size)])]
  transfers between devices with their start and end apart: 36 -> 35, of which waited for: 13 -> 18; matrix products, arithmetic and copies ran while one was open for 0% -> 0% of each run, Pallas kernels for 18% -> 16%
where the time goes in v3:
time: 104 us; the launch traced here: 102 us
  starting transfers between devices  47.8 us (46%)
  waiting for transfers between devices  33.1 us (32%)
  Pallas kernels  19.6 us (19%)
    ppermute x35, starting transfers between devices, send(): lax.ppermute(array, axis, [(i, (i + by) % size) for i in range(size)])  47.8 us
    ppermute x35, waiting for transfers between devices, send(): lax.ppermute(array, axis, [(i, (i + by) % size) for i in range(size)])  33.1 us
    pallas_call x2, Pallas kernels, dequant(): pl.pallas_call(functools.partial(dequant_kernel, by_row=by_row), grid=(de...  7 us
    pallas_call x2, Pallas kernels, decode(): pl.pallas_call(decode_kernel, in_specs=[IN_SMEM] + [IN_VMEM] * (Y + 1), o...  4.61 us
    pallas_call x2, Pallas kernels, encode(): pl.pallas_call(functools.partial(encode_kernel, pieces=len(pieces), chunk...  4.56 us
  transfers between devices with their start and end apart: 35, of which 18 were waited for; matrix products, arithmetic and copies ran while one was open for 0% of the time, Pallas kernels for 16%

profile of v3, /device:TPU:8, one launch (start us, length us, event | category | flops | bytes accessed | tf_op | source)
XLA Modules:
  0.0 102.1 jit_solution(6297996501690835300)
XLA Ops:
  0.6 6.4 %collective-permute-start.2 = (bf16[16,2304]{1,0:T(8,128)(2,1)}, bf16[16,2304]{1,0:T(8,128)(2,1)S(1)}, u32[]{:S(2)}, u32[]{:S(2)}) collective-permute-start(bf16[16,2304]{1,0:T(8,128)(2,1)} %bitcast.10), channel_id=1, source_target_pairs={{0,6},{2,0},{4,2},{6,4},{1,7},{3,1},{5,3},{7,5},{8,14},{10,8},{12,... | collective-permute-start | bytes 221192 | tf_op jit(solution)/shard_map/ppermute | solution.py:235
  7.0 3.8 %collective-permute-start = (bf16[16,2304]{1,0:T(8,128)(2,1)}, bf16[16,2304]{1,0:T(8,128)(2,1)S(1)}, u32[]{:S(2)}, u32[]{:S(2)}) collective-permute-start(bf16[16,2304]{1,0:T(8,128)(2,1)} %bitcast.12), channel_id=1, source_target_pairs={{0,4},{2,6},{4,0},{6,2},{1,5},{3,7},{5,1},{7,3},{8,12},{10,14},{12... | collective-permute-start | bytes 221192 | tf_op jit(solution)/shard_map/ppermute | solution.py:235
  11.6 3.5 %dequant.2.refs_8_ = bf16[2304,1280]{1,0:T(8,128)(2,1)S(1)} custom-call(f32[10,1,18]{2,1,0:T(1,128)S(1)} %bitcast.14, bf16[2304,1280]{1,0:T(8,128)(2,1)} %bitcast.16), custom_call_target="tpu_custom_call" | custom-call | flops 2949120 | bytes 11796480 | tf_op jit(solution)/shard_map/dequant/pallas_call | solution.py:73
  19.8 1.8 %collective-permute-start.3 = (bf16[64,2304]{1,0:T(8,128)(2,1)S(1)}, bf16[64,2304]{1,0:T(8,128)(2,1)S(1)}, u32[]{:S(2)}, u32[]{:S(2)}) collective-permute-start(bf16[64,2304]{1,0:T(8,128)(2,1)S(1)} %join.1.refs_0_), channel_id=1, source_target_pairs={{0,16},{8,24},{16,0},{24,8},{1,17},{9,25},{17,1},{25,9},{2,18},{10... | collective-permute-start | bytes 884744 | tf_op jit(solution)/shard_map/ppermute | solution.py:235
  21.6 3.5 %dequant.3.refs_4_ = bf16[1280,2304]{1,0:T(8,128)(2,1)S(1)} custom-call(f32[10,1,18]{2,1,0:T(1,128)S(1)} %bitcast.15, bf16[1280,2304]{1,0:T(8,128)(2,1)} %bitcast.17), custom_call_target="tpu_custom_call" | custom-call | flops 2949120 | bytes 11796480 | tf_op jit(solution)/shard_map/dequant/pallas_call | solution.py:73
  26.7 4.8 %collective-permute-done.4.refs_2_ = bf16[64,2304]{1,0:T(8,128)(2,1)S(1)} collective-permute-done((bf16[64,2304]{1,0:T(8,128)(2,1)S(1)}, bf16[64,2304]{1,0:T(8,128)(2,1)S(1)}, u32[]{:S(2)}, u32[]{:S(2)}) %collective-permute-start.4) | collective-permute-done | bytes 294944 | tf_op jit(solution)/shard_map/ppermute | solution.py:235
  35.7 2.3 %encode.2 = (bf16[64,1280]{1,0:T(8,128)(2,1)S(1)}, bf16[64,1280]{1,0:T(8,128)(2,1)S(1)}, bf16[64,1280]{1,0:T(8,128)(2,1)S(1)}, bf16[64,1280]{1,0:T(8,128)(2,1)S(1)}) custom-call(s32[4]{0:T(128)S(1)} %pad_add_fusion.where_ref, bf16[64,2304]{1,0:T(8,128)(2,1)S(1)} %join.1.refs_0_, bf16[64,2304]{1,0:T(8,128)(2,1)S(1)} %collective-permute-done.3.refs_1_, ...), custom_call_target="tpu_custom_call" | custom-call | flops 1509949440 | bytes 5898240 | tf_op jit(solution)/shard_map/encode/pallas_call | solution.py:111
  40.1 2.3 %collective-permute-start.12 = (bf16[64,1280]{1,0:T(8,128)(2,1)S(1)}, bf16[64,1280]{1,0:T(8,128)(2,1)S(1)}, u32[]{:S(2)}, u32[]{:S(2)}) collective-permute-start(bf16[64,1280]{1,0:T(8,128)(2,1)S(1)} %get-tuple-element.44), channel_id=1, source_target_pairs={{0,128},{64,192},{128,0},{192,64},{1,129},{65,193},{129,1},{193,65... | collective-permute-start | bytes 491528 | tf_op jit(solution)/shard_map/ppermute | solution.py:235
  42.4 2.3 %encode.3 = (bf16[64,1280]{1,0:T(8,128)(2,1)S(1)}, bf16[64,1280]{1,0:T(8,128)(2,1)S(1)}, bf16[64,1280]{1,0:T(8,128)(2,1)S(1)}, bf16[64,1280]{1,0:T(8,128)(2,1)S(1)}) custom-call(s32[4]{0:T(128)S(1)} %pad_add_fusion.where_ref, bf16[64,2304]{1,0:T(8,128)(2,1)S(1)} %join.1.refs_0_, bf16[64,2304]{1,0:T(8,128)(2,1)S(1)} %collective-permute-done.3.refs_1_, ...), custom_call_target="tpu_custom_call" | custom-call | flops 1509949440 | bytes 5898240 | tf_op jit(solution)/shard_map/encode/pallas_call | solution.py:111
  48.1 2.8 %collective-permute-done.12.refs_3_ = bf16[64,1280]{1,0:T(8,128)(2,1)S(1)} collective-permute-done((bf16[64,1280]{1,0:T(8,128)(2,1)S(1)}, bf16[64,1280]{1,0:T(8,128)(2,1)S(1)}, u32[]{:S(2)}, u32[]{:S(2)}) %collective-permute-start.12) | collective-permute-done | bytes 163872 | tf_op jit(solution)/shard_map/ppermute | solution.py:235
  52.4 1.9 %collective-permute-done.24.refs_2_ = bf16[64,1280]{1,0:T(8,128)(2,1)S(1)} collective-permute-done((bf16[64,1280]{1,0:T(8,128)(2,1)S(1)}, bf16[64,1280]{1,0:T(8,128)(2,1)S(1)}, u32[]{:S(2)}, u32[]{:S(2)}) %collective-permute-start.24) | collective-permute-done | bytes 163872 | tf_op jit(solution)/shard_map/ppermute | solution.py:235
  54.3 2.6 %collective-permute-done.25.refs_3_ = bf16[64,1280]{1,0:T(8,128)(2,1)S(1)} collective-permute-done((bf16[64,1280]{1,0:T(8,128)(2,1)S(1)}, bf16[64,1280]{1,0:T(8,128)(2,1)S(1)}, u32[]{:S(2)}, u32[]{:S(2)}) %collective-permute-start.25) | collective-permute-done | bytes 163872 | tf_op jit(solution)/shard_map/ppermute | solution.py:235
  57.2 2.0 %collective-permute-start.15 = (bf16[64,1280]{1,0:T(8,128)(2,1)S(1)}, bf16[64,1280]{1,0:T(8,128)(2,1)S(1)}, u32[]{:S(2)}, u32[]{:S(2)}) collective-permute-start(bf16[64,1280]{1,0:T(8,128)(2,1)S(1)} %activate.2.refs_0_), channel_id=1, source_target_pairs={{0,192},{64,0},{128,64},{192,128},{1,193},{65,1},{129,65},{193,129... | collective-permute-start | bytes 491528 | tf_op jit(solution)/shard_map/ppermute | solution.py:235
  66.3 3.3 %collective-permute-done.14.refs_1_ = bf16[64,1280]{1,0:T(8,128)(2,1)S(1)} collective-permute-done((bf16[64,1280]{1,0:T(8,128)(2,1)S(1)}, bf16[64,1280]{1,0:T(8,128)(2,1)S(1)}, u32[]{:S(2)}, u32[]{:S(2)}) %collective-permute-start.14) | collective-permute-done | bytes 163872 | tf_op jit(solution)/shard_map/ppermute | solution.py:235
  69.6 2.3 %decode.2 = (bf16[128,2304]{1,0:T(8,128)(2,1)S(1)}, bf16[128,2304]{1,0:T(8,128)(2,1)S(1)}) custom-call(s32[4]{0:T(128)S(1)} %pad_add_fusion.where_ref, bf16[64,1280]{1,0:T(8,128)(2,1)S(1)} %activate.2.refs_0_, bf16[64,1280]{1,0:T(8,128)(2,1)S(1)} %collective-permute-done.14.refs_1_, bf16[64,1280]{1,0:T(8,128)(2,1)S(1)} %collective-permute-done.15.refs_2_, ...), custom_call_target="tpu_custom_call" | custom-call | flops 1509949440 | bytes 5898240 | tf_op jit(solution)/shard_map/decode/pallas_call | solution.py:141
  72.1 2.0 %collective-permute-done.27.refs_1_.refs_5_ = bf16[64,1280]{1,0:T(8,128)(2,1)S(1)} collective-permute-done((bf16[64,1280]{1,0:T(8,128)(2,1)S(1)}, bf16[64,1280]{1,0:T(8,128)(2,1)S(1)}, u32[]{:S(2)}, u32[]{:S(2)}) %collective-permute-start.27) | collective-permute-done | bytes 163872 | tf_op jit(solution)/shard_map/ppermute | solution.py:235
  74.1 2.3 %decode.3 = (bf16[128,2304]{1,0:T(8,128)(2,1)S(1)}, bf16[128,2304]{1,0:T(8,128)(2,1)S(1)}) custom-call(s32[4]{0:T(128)S(1)} %pad_add_fusion.where_ref, bf16[64,1280]{1,0:T(8,128)(2,1)S(1)} %activate.3.refs_0_.refs_4_, bf16[64,1280]{1,0:T(8,128)(2,1)S(1)} %collective-permute-done.27.refs_1_.refs_5_, ...), custom_call_target="tpu_custom_call" | custom-call | flops 1509949440 | bytes 5898240 | tf_op jit(solution)/shard_map/decode/pallas_call | solution.py:141
  77.9 2.1 %collective-permute-start.19 = (bf16[32,2304]{1,0:T(8,128)(2,1)S(1)}, bf16[32,2304]{1,0:T(8,128)(2,1)S(1)}, u32[]{:S(2)}, u32[]{:S(2)}) collective-permute-start(bf16[32,2304]{1,0:T(8,128)(2,1)S(1)} %get-tuple-element.49), channel_id=1, source_target_pairs={{0,24},{8,0},{16,8},{24,16},{1,25},{9,1},{17,9},{25,17},{2,26},{10... | collective-permute-start | bytes 442376 | tf_op jit(solution)/shard_map/ppermute | solution.py:235
  80.2 4.1 %collective-permute-done.18.refs_1_ = bf16[32,2304]{1,0:T(8,128)(2,1)S(1)} collective-permute-done((bf16[32,2304]{1,0:T(8,128)(2,1)S(1)}, bf16[32,2304]{1,0:T(8,128)(2,1)S(1)}, u32[]{:S(2)}, u32[]{:S(2)}) %collective-permute-start.18) | collective-permute-done | bytes 147488 | tf_op jit(solution)/shard_map/ppermute | solution.py:235
  84.8 3.0 %collective-permute-start.32 = (bf16[32,2304]{1,0:T(8,128)(2,1)S(1)}, bf16[32,2304]{1,0:T(8,128)(2,1)S(1)}, u32[]{:S(2)}, u32[]{:S(2)}) collective-permute-start(bf16[32,2304]{1,0:T(8,128)(2,1)S(1)} %get-tuple-element.64), channel_id=1, source_target_pairs={{0,24},{8,0},{16,8},{24,16},{1,25},{9,1},{17,9},{25,17},{2,26},{10... | collective-permute-start | bytes 442376 | tf_op jit(solution)/shard_map/ppermute | solution.py:235
  88.2 2.7 %collective-permute-start.21 = (bf16[16,2304]{1,0:T(8,128)(2,1)S(1)}, bf16[16,2304]{1,0:T(8,128)(2,1)S(1)}, u32[]{:S(2)}, u32[]{:S(2)}) collective-permute-start(bf16[16,2304]{1,0:T(8,128)(2,1)S(1)} %get-tuple-element.51), channel_id=1, source_target_pairs={{0,4},{2,6},{4,0},{6,2},{1,5},{3,7},{5,1},{7,3},{8,12},{10,14},{12... | collective-permute-start | bytes 221192 | tf_op jit(solution)/shard_map/ppermute | solution.py:235
  90.9 3.9 %collective-permute-start.22 = (bf16[16,2304]{1,0:T(8,128)(2,1)S(1)}, bf16[16,2304]{1,0:T(8,128)(2,1)S(1)}, u32[]{:S(2)}, u32[]{:S(2)}) collective-permute-start(bf16[16,2304]{1,0:T(8,128)(2,1)S(1)} %get-tuple-element.52), channel_id=1, source_target_pairs={{0,6},{2,0},{4,2},{6,4},{1,7},{3,1},{5,3},{7,5},{8,14},{10,8},{12,... | collective-permute-start | bytes 221192 | tf_op jit(solution)/shard_map/ppermute | solution.py:235
  94.9 2.6 %collective-permute-start.34 = (bf16[16,2304]{1,0:T(8,128)(2,1)S(1)}, bf16[16,2304]{1,0:T(8,128)(2,1)S(1)}, u32[]{:S(2)}, u32[]{:S(2)}) collective-permute-start(bf16[16,2304]{1,0:T(8,128)(2,1)S(1)} %get-tuple-element.67), channel_id=1, source_target_pairs={{0,2},{2,4},{4,6},{6,0},{1,3},{3,5},{5,7},{7,1},{8,10},{10,12},{12... | collective-permute-start | bytes 221192 | tf_op jit(solution)/shard_map/ppermute | solution.py:235
  97.5 2.0 %place.1 = bf16[512,1280]{1,0:T(8,128)(2,1)} custom-call(s32[4]{0:T(128)S(1)} %pad_add_fusion.where_ref, bf16[64,1280]{1,0:T(8,128)(2,1)S(1)} %activate.2.refs_0_, bf16[64,1280]{1,0:T(8,128)(2,1)S(1)} %collective-permute-done.14.refs_1_, bf16[64,1280]{1,0:T(8,128)(2,1)S(1)} %collective-permute-done.15.refs_2_, ...), custom_call_target="tpu_custom_call" | custom-call | bytes 2621440 | tf_op jit(solution)/shard_map/place/pallas_call | solution.py:218
  (74 shorter events, 31.0 us)
Async XLA Ops:
  0.6 14.5 %collective-permute-start.2 = (bf16[16,2304]{1,0:T(8,128)(2,1)}, bf16[16,2304]{1,0:T(8,128)(2,1)S(1)}, u32[]{:S(2)}, u32[]{:S(2)}) collective-permute-start(bf16[16,2304]{1,0:T(8,128)(2,1)} %bitcast.10), channel_id=1, source_target_pairs={{0,6},{2,0},{4,2},{6,4},{1,7},{3,1},{5,3},{7,5},{8,14},{10,8},{12,... | collective-permute-start | bytes 221192 | tf_op jit(solution)/shard_map/ppermute | solution.py:235
  7.0 9.4 %collective-permute-start.1 = (bf16[16,2304]{1,0:T(8,128)(2,1)}, bf16[16,2304]{1,0:T(8,128)(2,1)S(1)}, u32[]{:S(2)}, u32[]{:S(2)}) collective-permute-start(bf16[16,2304]{1,0:T(8,128)(2,1)} %bitcast.11), channel_id=1, source_target_pairs={{0,2},{2,4},{4,6},{6,0},{1,3},{3,5},{5,7},{7,1},{8,10},{10,12},{12... | collective-permute-start | bytes 221192 | tf_op jit(solution)/shard_map/ppermute | solution.py:235
  7.0 9.4 %collective-permute-start = (bf16[16,2304]{1,0:T(8,128)(2,1)}, bf16[16,2304]{1,0:T(8,128)(2,1)S(1)}, u32[]{:S(2)}, u32[]{:S(2)}) collective-permute-start(bf16[16,2304]{1,0:T(8,128)(2,1)} %bitcast.12), channel_id=1, source_target_pairs={{0,4},{2,6},{4,0},{6,2},{1,5},{3,7},{5,1},{7,3},{8,12},{10,14},{12... | collective-permute-start | bytes 221192 | tf_op jit(solution)/shard_map/ppermute | solution.py:235
  16.5 10.2 %collective-permute-start.5 = (bf16[64,2304]{1,0:T(8,128)(2,1)S(1)}, bf16[64,2304]{1,0:T(8,128)(2,1)S(1)}, u32[]{:S(2)}, u32[]{:S(2)}) collective-permute-start(bf16[64,2304]{1,0:T(8,128)(2,1)S(1)} %join.1.refs_0_), channel_id=1, source_target_pairs={{0,8},{8,16},{16,24},{24,0},{1,9},{9,17},{17,25},{25,1},{2,10},{10... | collective-permute-start | bytes 884744 | tf_op jit(solution)/shard_map/ppermute | solution.py:235
  18.1 13.5 %collective-permute-start.4 = (bf16[64,2304]{1,0:T(8,128)(2,1)S(1)}, bf16[64,2304]{1,0:T(8,128)(2,1)S(1)}, u32[]{:S(2)}, u32[]{:S(2)}) collective-permute-start(bf16[64,2304]{1,0:T(8,128)(2,1)S(1)} %join.1.refs_0_), channel_id=1, source_target_pairs={{0,24},{8,0},{16,8},{24,16},{1,25},{9,1},{17,9},{25,17},{2,26},{10... | collective-permute-start | bytes 884744 | tf_op jit(solution)/shard_map/ppermute | solution.py:235
  19.8 13.4 %collective-permute-start.3 = (bf16[64,2304]{1,0:T(8,128)(2,1)S(1)}, bf16[64,2304]{1,0:T(8,128)(2,1)S(1)}, u32[]{:S(2)}, u32[]{:S(2)}) collective-permute-start(bf16[64,2304]{1,0:T(8,128)(2,1)S(1)} %join.1.refs_0_), channel_id=1, source_target_pairs={{0,16},{8,24},{16,0},{24,8},{1,17},{9,25},{17,1},{25,9},{2,18},{10... | collective-permute-start | bytes 884744 | tf_op jit(solution)/shard_map/ppermute | solution.py:235
  21.6 12.1 %collective-permute-start.6 = (bf16[64,2304]{1,0:T(8,128)(2,1)S(1)}, bf16[64,2304]{1,0:T(8,128)(2,1)S(1)}, u32[]{:S(2)}, u32[]{:S(2)}) collective-permute-start(bf16[64,2304]{1,0:T(8,128)(2,1)S(1)} %join.1.refs_0_), channel_id=1, source_target_pairs={{0,1},{1,0},{2,3},{3,2},{4,5},{5,4},{6,7},{7,6},{8,9},{9,8},{10,11... | collective-permute-start | bytes 884744 | tf_op jit(solution)/shard_map/ppermute | solution.py:235
  38.0 8.8 %collective-permute-start.10 = (bf16[64,1280]{1,0:T(8,128)(2,1)S(1)}, bf16[64,1280]{1,0:T(8,128)(2,1)S(1)}, u32[]{:S(2)}, u32[]{:S(2)}) collective-permute-start(bf16[64,1280]{1,0:T(8,128)(2,1)S(1)} %get-tuple-element.42), channel_id=1, source_target_pairs={{0,64},{64,128},{128,192},{192,0},{1,65},{65,129},{129,193},{193,1... | collective-permute-start | bytes 491528 | tf_op jit(solution)/shard_map/ppermute | solution.py:235
  39.6 8.5 %collective-permute-start.11 = (bf16[64,1280]{1,0:T(8,128)(2,1)S(1)}, bf16[64,1280]{1,0:T(8,128)(2,1)S(1)}, u32[]{:S(2)}, u32[]{:S(2)}) collective-permute-start(bf16[64,1280]{1,0:T(8,128)(2,1)S(1)} %get-tuple-element.43), channel_id=1, source_target_pairs={{0,192},{64,0},{128,64},{192,128},{1,193},{65,1},{129,65},{193,129... | collective-permute-start | bytes 491528 | tf_op jit(solution)/shard_map/ppermute | solution.py:235
  40.1 10.9 %collective-permute-start.12 = (bf16[64,1280]{1,0:T(8,128)(2,1)S(1)}, bf16[64,1280]{1,0:T(8,128)(2,1)S(1)}, u32[]{:S(2)}, u32[]{:S(2)}) collective-permute-start(bf16[64,1280]{1,0:T(8,128)(2,1)S(1)} %get-tuple-element.44), channel_id=1, source_target_pairs={{0,128},{64,192},{128,0},{192,64},{1,129},{65,193},{129,1},{193,65... | collective-permute-start | bytes 491528 | tf_op jit(solution)/shard_map/ppermute | solution.py:235
  44.6 7.7 %collective-permute-start.23 = (bf16[64,1280]{1,0:T(8,128)(2,1)S(1)}, bf16[64,1280]{1,0:T(8,128)(2,1)S(1)}, u32[]{:S(2)}, u32[]{:S(2)}) collective-permute-start(bf16[64,1280]{1,0:T(8,128)(2,1)S(1)} %get-tuple-element.55), channel_id=1, source_target_pairs={{0,64},{64,128},{128,192},{192,0},{1,65},{65,129},{129,193},{193,1... | collective-permute-start | bytes 491528 | tf_op jit(solution)/shard_map/ppermute | solution.py:235
  45.5 8.7 %collective-permute-start.24 = (bf16[64,1280]{1,0:T(8,128)(2,1)S(1)}, bf16[64,1280]{1,0:T(8,128)(2,1)S(1)}, u32[]{:S(2)}, u32[]{:S(2)}) collective-permute-start(bf16[64,1280]{1,0:T(8,128)(2,1)S(1)} %get-tuple-element.56), channel_id=1, source_target_pairs={{0,192},{64,0},{128,64},{192,128},{1,193},{65,1},{129,65},{193,129... | collective-permute-start | bytes 491528 | tf_op jit(solution)/shard_map/ppermute | solution.py:235
  46.7 10.1 %collective-permute-start.25 = (bf16[64,1280]{1,0:T(8,128)(2,1)S(1)}, bf16[64,1280]{1,0:T(8,128)(2,1)S(1)}, u32[]{:S(2)}, u32[]{:S(2)}) collective-permute-start(bf16[64,1280]{1,0:T(8,128)(2,1)S(1)} %get-tuple-element.57), channel_id=1, source_target_pairs={{0,128},{64,192},{128,0},{192,64},{1,129},{65,193},{129,1},{193,65... | collective-permute-start | bytes 491528 | tf_op jit(solution)/shard_map/ppermute | solution.py:235
  57.2 9.0 %collective-permute-start.15 = (bf16[64,1280]{1,0:T(8,128)(2,1)S(1)}, bf16[64,1280]{1,0:T(8,128)(2,1)S(1)}, u32[]{:S(2)}, u32[]{:S(2)}) collective-permute-start(bf16[64,1280]{1,0:T(8,128)(2,1)S(1)} %activate.2.refs_0_), channel_id=1, source_target_pairs={{0,192},{64,0},{128,64},{192,128},{1,193},{65,1},{129,65},{193,129... | collective-permute-start | bytes 491528 | tf_op jit(solution)/shard_map/ppermute | solution.py:235
  59.2 10.4 %collective-permute-start.14 = (bf16[64,1280]{1,0:T(8,128)(2,1)S(1)}, bf16[64,1280]{1,0:T(8,128)(2,1)S(1)}, u32[]{:S(2)}, u32[]{:S(2)}) collective-permute-start(bf16[64,1280]{1,0:T(8,128)(2,1)S(1)} %activate.2.refs_0_), channel_id=1, source_target_pairs={{0,128},{64,192},{128,0},{192,64},{1,129},{65,193},{129,1},{193,65... | collective-permute-start | bytes 491528 | tf_op jit(solution)/shard_map/ppermute | solution.py:235
  62.4 9.6 %collective-permute-start.29 = (bf16[64,1280]{1,0:T(8,128)(2,1)S(1)}, bf16[64,1280]{1,0:T(8,128)(2,1)S(1)}, u32[]{:S(2)}, u32[]{:S(2)}) collective-permute-start(bf16[64,1280]{1,0:T(8,128)(2,1)S(1)} %activate.3.refs_0_.refs_4_), channel_id=1, source_target_pairs={{0,64},{64,128},{128,192},{192,0},{1,65},{65,129},{129,193},{193,1... | collective-permute-start | bytes 491528 | tf_op jit(solution)/shard_map/ppermute | solution.py:235
  62.9 9.1 %collective-permute-start.28 = (bf16[64,1280]{1,0:T(8,128)(2,1)S(1)}, bf16[64,1280]{1,0:T(8,128)(2,1)S(1)}, u32[]{:S(2)}, u32[]{:S(2)}) collective-permute-start(bf16[64,1280]{1,0:T(8,128)(2,1)S(1)} %activate.3.refs_0_.refs_4_), channel_id=1, source_target_pairs={{0,192},{64,0},{128,64},{192,128},{1,193},{65,1},{129,65},{193,129... | collective-permute-start | bytes 491528 | tf_op jit(solution)/shard_map/ppermute | solution.py:235
  64.5 9.6 %collective-permute-start.27 = (bf16[64,1280]{1,0:T(8,128)(2,1)S(1)}, bf16[64,1280]{1,0:T(8,128)(2,1)S(1)}, u32[]{:S(2)}, u32[]{:S(2)}) collective-permute-start(bf16[64,1280]{1,0:T(8,128)(2,1)S(1)} %activate.3.refs_0_.refs_4_), channel_id=1, source_target_pairs={{0,128},{64,192},{128,0},{192,64},{1,129},{65,193},{129,1},{193,65... | collective-permute-start | bytes 491528 | tf_op jit(solution)/shard_map/ppermute | solution.py:235
  77.9 9.8 %collective-permute-start.19 = (bf16[32,2304]{1,0:T(8,128)(2,1)S(1)}, bf16[32,2304]{1,0:T(8,128)(2,1)S(1)}, u32[]{:S(2)}, u32[]{:S(2)}) collective-permute-start(bf16[32,2304]{1,0:T(8,128)(2,1)S(1)} %get-tuple-element.49), channel_id=1, source_target_pairs={{0,24},{8,0},{16,8},{24,16},{1,25},{9,1},{17,9},{25,17},{2,26},{10... | collective-permute-start | bytes 442376 | tf_op jit(solution)/shard_map/ppermute | solution.py:235
  80.0 8.1 %collective-permute-start.20 = (bf16[32,2304]{1,0:T(8,128)(2,1)S(1)}, bf16[32,2304]{1,0:T(8,128)(2,1)S(1)}, u32[]{:S(2)}, u32[]{:S(2)}) collective-permute-start(bf16[32,2304]{1,0:T(8,128)(2,1)S(1)} %get-tuple-element.50), channel_id=1, source_target_pairs={{0,16},{8,24},{16,0},{24,8},{1,17},{9,25},{17,1},{25,9},{2,18},{10... | collective-permute-start | bytes 442376 | tf_op jit(solution)/shard_map/ppermute | solution.py:235
  84.4 10.3 %collective-permute-start.31 = (bf16[32,2304]{1,0:T(8,128)(2,1)S(1)}, bf16[32,2304]{1,0:T(8,128)(2,1)S(1)}, u32[]{:S(2)}, u32[]{:S(2)}) collective-permute-start(bf16[32,2304]{1,0:T(8,128)(2,1)S(1)} %get-tuple-element.63), channel_id=1, source_target_pairs={{0,8},{8,16},{16,24},{24,0},{1,9},{9,17},{17,25},{25,1},{2,10},{10... | collective-permute-start | bytes 442376 | tf_op jit(solution)/shard_map/ppermute | solution.py:235
  84.8 10.0 %collective-permute-start.32 = (bf16[32,2304]{1,0:T(8,128)(2,1)S(1)}, bf16[32,2304]{1,0:T(8,128)(2,1)S(1)}, u32[]{:S(2)}, u32[]{:S(2)}) collective-permute-start(bf16[32,2304]{1,0:T(8,128)(2,1)S(1)} %get-tuple-element.64), channel_id=1, source_target_pairs={{0,24},{8,0},{16,8},{24,16},{1,25},{9,1},{17,9},{25,17},{2,26},{10... | collective-permute-start | bytes 442376 | tf_op jit(solution)/shard_map/ppermute | solution.py:235
  88.2 11.3 %collective-permute-start.21 = (bf16[16,2304]{1,0:T(8,128)(2,1)S(1)}, bf16[16,2304]{1,0:T(8,128)(2,1)S(1)}, u32[]{:S(2)}, u32[]{:S(2)}) collective-permute-start(bf16[16,2304]{1,0:T(8,128)(2,1)S(1)} %get-tuple-element.51), channel_id=1, source_target_pairs={{0,4},{2,6},{4,0},{6,2},{1,5},{3,7},{5,1},{7,3},{8,12},{10,14},{12... | collective-permute-start | bytes 221192 | tf_op jit(solution)/shard_map/ppermute | solution.py:235
  90.9 9.0 %collective-permute-start.22 = (bf16[16,2304]{1,0:T(8,128)(2,1)S(1)}, bf16[16,2304]{1,0:T(8,128)(2,1)S(1)}, u32[]{:S(2)}, u32[]{:S(2)}) collective-permute-start(bf16[16,2304]{1,0:T(8,128)(2,1)S(1)} %get-tuple-element.52), channel_id=1, source_target_pairs={{0,6},{2,0},{4,2},{6,4},{1,7},{3,1},{5,3},{7,5},{8,14},{10,8},{12,... | collective-permute-start | bytes 221192 | tf_op jit(solution)/shard_map/ppermute | solution.py:235
  (16 other events, 118.0 us)

commit v4 on v3

--- a/solution.py
+++ b/solution.py
@@ -10,8 +10,8 @@
 BLOCK = 128
 Y, ZL, X, ZH, C = 4, 2, 4, 4, 2
 LAYER, LAT = ("y", "zl"), ("x", "zh", "c")
-ORDER = (0, 2, 1, 3)
-SENT = (2, 3, 1)
+ORDER = (0, 1, 3, 2)
+SENT = (1, 2, 3)
 F32, BF16 = jnp.float32, jnp.bfloat16
 MIB = 1 << 20
 IN_VMEM = pl.BlockSpec(memory_space=pltpu.VMEM)
@@ -197,7 +197,7 @@
         for j in range(blocks):
             b = quarter * blocks + j
             kc, p, k = b // (2 * X), lax.rem(b // 2, X), lax.rem(b, 2)
-            kx = jnp.where(p == 1, ORDER[1], jnp.where(p == 2, ORDER[2], p))
+            kx = jnp.where(p == 1, ORDER[1], jnp.where(p == 2, ORDER[2], jnp.where(p == 3, ORDER[3], 0)))
             owner = (lax.rem(x + kx, X) * ZH + lax.rem(zh + 2 * (1 - n) + k, ZH)) * C + lax.rem(c + kc, C)
             copies.append(
                 pltpu.make_async_copy(

time: 104 us -> 104 us (level); the launches traced: 102 us -> 103 us
    ppermute x35, starting transfers between devices: 47.8 us -> 48.8 us  [send(): lax.ppermute(array, axis, [(i, (i + by) % size) for i in range(size)])]
  transfers between devices with their start and end apart: 35 -> 35, of which waited for: 18 -> 20; matrix products, arithmetic and copies ran while one was open for 0% -> 0% of each run, Pallas kernels for 16% -> 16%
where the time goes in v4:
time: 104 us; the launch traced here: 103 us
  starting transfers between devices  48.8 us (47%)
  waiting for transfers between devices  33.3 us (32%)
  Pallas kernels  19.6 us (19%)
    ppermute x35, starting transfers between devices, send(): lax.ppermute(array, axis, [(i, (i + by) % size) for i in range(size)])  48.8 us
    ppermute x35, waiting for transfers between devices, send(): lax.ppermute(array, axis, [(i, (i + by) % size) for i in range(size)])  33.3 us
    pallas_call x2, Pallas kernels, dequant(): pl.pallas_call(functools.partial(dequant_kernel, by_row=by_row), grid=(de...  7 us
    pallas_call x2, Pallas kernels, decode(): pl.pallas_call(decode_kernel, in_specs=[IN_SMEM] + [IN_VMEM] * (Y + 1), o...  4.61 us
    pallas_call x2, Pallas kernels, encode(): pl.pallas_call(functools.partial(encode_kernel, pieces=len(pieces), chunk...  4.55 us
  transfers between devices with their start and end apart: 35, of which 20 were waited for; matrix products, arithmetic and copies ran while one was open for 0% of the time, Pallas kernels for 16%

profile of v4, /device:TPU:8, one launch (start us, length us, event | category | flops | bytes accessed | tf_op | source)
XLA Modules:
  0.0 103.4 jit_solution(16685401881221720923)
XLA Ops:
  0.6 6.4 %collective-permute-start.2 = (bf16[16,2304]{1,0:T(8,128)(2,1)}, bf16[16,2304]{1,0:T(8,128)(2,1)S(1)}, u32[]{:S(2)}, u32[]{:S(2)}) collective-permute-start(bf16[16,2304]{1,0:T(8,128)(2,1)} %bitcast.10), channel_id=1, source_target_pairs={{0,6},{2,0},{4,2},{6,4},{1,7},{3,1},{5,3},{7,5},{8,14},{10,8},{12,... | collective-permute-start | bytes 221192 | tf_op jit(solution)/shard_map/ppermute | solution.py:235
  7.0 3.8 %collective-permute-start = (bf16[16,2304]{1,0:T(8,128)(2,1)}, bf16[16,2304]{1,0:T(8,128)(2,1)S(1)}, u32[]{:S(2)}, u32[]{:S(2)}) collective-permute-start(bf16[16,2304]{1,0:T(8,128)(2,1)} %bitcast.12), channel_id=1, source_target_pairs={{0,4},{2,6},{4,0},{6,2},{1,5},{3,7},{5,1},{7,3},{8,12},{10,14},{12... | collective-permute-start | bytes 221192 | tf_op jit(solution)/shard_map/ppermute | solution.py:235
  11.6 3.5 %dequant.2.refs_8_ = bf16[2304,1280]{1,0:T(8,128)(2,1)S(1)} custom-call(f32[10,1,18]{2,1,0:T(1,128)S(1)} %bitcast.14, bf16[2304,1280]{1,0:T(8,128)(2,1)} %bitcast.16), custom_call_target="tpu_custom_call" | custom-call | flops 2949120 | bytes 11796480 | tf_op jit(solution)/shard_map/dequant/pallas_call | solution.py:73
  16.5 3.1 %collective-permute-start.5 = (bf16[64,2304]{1,0:T(8,128)(2,1)S(1)}, bf16[64,2304]{1,0:T(8,128)(2,1)S(1)}, u32[]{:S(2)}, u32[]{:S(2)}) collective-permute-start(bf16[64,2304]{1,0:T(8,128)(2,1)S(1)} %join.1.refs_0_), channel_id=1, source_target_pairs={{0,16},{8,24},{16,0},{24,8},{1,17},{9,25},{17,1},{25,9},{2,18},{10... | collective-permute-start | bytes 884744 | tf_op jit(solution)/shard_map/ppermute | solution.py:235
  20.2 2.6 %collective-permute-start.3 = (bf16[64,2304]{1,0:T(8,128)(2,1)S(1)}, bf16[64,2304]{1,0:T(8,128)(2,1)S(1)}, u32[]{:S(2)}, u32[]{:S(2)}) collective-permute-start(bf16[64,2304]{1,0:T(8,128)(2,1)S(1)} %join.1.refs_0_), channel_id=1, source_target_pairs={{0,24},{8,0},{16,8},{24,16},{1,25},{9,1},{17,9},{25,17},{2,26},{10... | collective-permute-start | bytes 884744 | tf_op jit(solution)/shard_map/ppermute | solution.py:235
  22.8 3.5 %dequant.3.refs_4_ = bf16[1280,2304]{1,0:T(8,128)(2,1)S(1)} custom-call(f32[10,1,18]{2,1,0:T(1,128)S(1)} %bitcast.15, bf16[1280,2304]{1,0:T(8,128)(2,1)} %bitcast.17), custom_call_target="tpu_custom_call" | custom-call | flops 2949120 | bytes 11796480 | tf_op jit(solution)/shard_map/dequant/pallas_call | solution.py:73
  28.1 4.5 %collective-permute-done.4.refs_2_ = bf16[64,2304]{1,0:T(8,128)(2,1)S(1)} collective-permute-done((bf16[64,2304]{1,0:T(8,128)(2,1)S(1)}, bf16[64,2304]{1,0:T(8,128)(2,1)S(1)}, u32[]{:S(2)}, u32[]{:S(2)}) %collective-permute-start.4) | collective-permute-done | bytes 294944 | tf_op jit(solution)/shard_map/ppermute | solution.py:235
  35.1 2.3 %encode.2 = (bf16[64,1280]{1,0:T(8,128)(2,1)S(1)}, bf16[64,1280]{1,0:T(8,128)(2,1)S(1)}, bf16[64,1280]{1,0:T(8,128)(2,1)S(1)}, bf16[64,1280]{1,0:T(8,128)(2,1)S(1)}) custom-call(s32[4]{0:T(128)S(1)} %pad_add_fusion.where_ref, bf16[64,2304]{1,0:T(8,128)(2,1)S(1)} %join.1.refs_0_, bf16[64,2304]{1,0:T(8,128)(2,1)S(1)} %collective-permute-done.3.refs_1_, ...), custom_call_target="tpu_custom_call" | custom-call | flops 1509949440 | bytes 5898240 | tf_op jit(solution)/shard_map/encode/pallas_call | solution.py:111
  39.5 2.3 %collective-permute-start.12 = (bf16[64,1280]{1,0:T(8,128)(2,1)S(1)}, bf16[64,1280]{1,0:T(8,128)(2,1)S(1)}, u32[]{:S(2)}, u32[]{:S(2)}) collective-permute-start(bf16[64,1280]{1,0:T(8,128)(2,1)S(1)} %get-tuple-element.44), channel_id=1, source_target_pairs={{0,128},{64,192},{128,0},{192,64},{1,129},{65,193},{129,1},{193,65... | collective-permute-start | bytes 491528 | tf_op jit(solution)/shard_map/ppermute | solution.py:235
  41.8 2.3 %encode.3 = (bf16[64,1280]{1,0:T(8,128)(2,1)S(1)}, bf16[64,1280]{1,0:T(8,128)(2,1)S(1)}, bf16[64,1280]{1,0:T(8,128)(2,1)S(1)}, bf16[64,1280]{1,0:T(8,128)(2,1)S(1)}) custom-call(s32[4]{0:T(128)S(1)} %pad_add_fusion.where_ref, bf16[64,2304]{1,0:T(8,128)(2,1)S(1)} %join.1.refs_0_, bf16[64,2304]{1,0:T(8,128)(2,1)S(1)} %collective-permute-done.3.refs_1_, ...), custom_call_target="tpu_custom_call" | custom-call | flops 1509949440 | bytes 5898240 | tf_op jit(solution)/shard_map/encode/pallas_call | solution.py:111
  47.6 2.8 %collective-permute-done.12.refs_3_ = bf16[64,1280]{1,0:T(8,128)(2,1)S(1)} collective-permute-done((bf16[64,1280]{1,0:T(8,128)(2,1)S(1)}, bf16[64,1280]{1,0:T(8,128)(2,1)S(1)}, u32[]{:S(2)}, u32[]{:S(2)}) %collective-permute-start.12) | collective-permute-done | bytes 163872 | tf_op jit(solution)/shard_map/ppermute | solution.py:235
  51.8 1.9 %collective-permute-done.24.refs_2_ = bf16[64,1280]{1,0:T(8,128)(2,1)S(1)} collective-permute-done((bf16[64,1280]{1,0:T(8,128)(2,1)S(1)}, bf16[64,1280]{1,0:T(8,128)(2,1)S(1)}, u32[]{:S(2)}, u32[]{:S(2)}) %collective-permute-start.24) | collective-permute-done | bytes 163872 | tf_op jit(solution)/shard_map/ppermute | solution.py:235
  53.7 2.6 %collective-permute-done.25.refs_3_ = bf16[64,1280]{1,0:T(8,128)(2,1)S(1)} collective-permute-done((bf16[64,1280]{1,0:T(8,128)(2,1)S(1)}, bf16[64,1280]{1,0:T(8,128)(2,1)S(1)}, u32[]{:S(2)}, u32[]{:S(2)}) %collective-permute-start.25) | collective-permute-done | bytes 163872 | tf_op jit(solution)/shard_map/ppermute | solution.py:235
  56.6 1.8 %collective-permute-start.16 = (bf16[64,1280]{1,0:T(8,128)(2,1)S(1)}, bf16[64,1280]{1,0:T(8,128)(2,1)S(1)}, u32[]{:S(2)}, u32[]{:S(2)}) collective-permute-start(bf16[64,1280]{1,0:T(8,128)(2,1)S(1)} %activate.2.refs_0_), channel_id=1, source_target_pairs={{0,128},{64,192},{128,0},{192,64},{1,129},{65,193},{129,1},{193,65... | collective-permute-start | bytes 491528 | tf_op jit(solution)/shard_map/ppermute | solution.py:235
  66.9 2.8 %collective-permute-done.14.refs_1_ = bf16[64,1280]{1,0:T(8,128)(2,1)S(1)} collective-permute-done((bf16[64,1280]{1,0:T(8,128)(2,1)S(1)}, bf16[64,1280]{1,0:T(8,128)(2,1)S(1)}, u32[]{:S(2)}, u32[]{:S(2)}) %collective-permute-start.14) | collective-permute-done | bytes 163872 | tf_op jit(solution)/shard_map/ppermute | solution.py:235
  69.7 2.3 %decode.2 = (bf16[128,2304]{1,0:T(8,128)(2,1)S(1)}, bf16[128,2304]{1,0:T(8,128)(2,1)S(1)}) custom-call(s32[4]{0:T(128)S(1)} %pad_add_fusion.where_ref, bf16[64,1280]{1,0:T(8,128)(2,1)S(1)} %activate.2.refs_0_, bf16[64,1280]{1,0:T(8,128)(2,1)S(1)} %collective-permute-done.14.refs_1_, bf16[64,1280]{1,0:T(8,128)(2,1)S(1)} %collective-permute-done.15.refs_2_, ...), custom_call_target="tpu_custom_call" | custom-call | flops 1509949440 | bytes 5898240 | tf_op jit(solution)/shard_map/decode/pallas_call | solution.py:141
  73.8 2.3 %decode.3 = (bf16[128,2304]{1,0:T(8,128)(2,1)S(1)}, bf16[128,2304]{1,0:T(8,128)(2,1)S(1)}) custom-call(s32[4]{0:T(128)S(1)} %pad_add_fusion.where_ref, bf16[64,1280]{1,0:T(8,128)(2,1)S(1)} %activate.3.refs_0_.refs_4_, bf16[64,1280]{1,0:T(8,128)(2,1)S(1)} %collective-permute-done.27.refs_1_.refs_5_, ...), custom_call_target="tpu_custom_call" | custom-call | flops 1509949440 | bytes 5898240 | tf_op jit(solution)/shard_map/decode/pallas_call | solution.py:141
  80.5 3.4 %collective-permute-done.18.refs_1_ = bf16[32,2304]{1,0:T(8,128)(2,1)S(1)} collective-permute-done((bf16[32,2304]{1,0:T(8,128)(2,1)S(1)}, bf16[32,2304]{1,0:T(8,128)(2,1)S(1)}, u32[]{:S(2)}, u32[]{:S(2)}) %collective-permute-start.18) | collective-permute-done | bytes 147488 | tf_op jit(solution)/shard_map/ppermute | solution.py:235
  84.8 2.6 %collective-permute-start.32 = (bf16[32,2304]{1,0:T(8,128)(2,1)S(1)}, bf16[32,2304]{1,0:T(8,128)(2,1)S(1)}, u32[]{:S(2)}, u32[]{:S(2)}) collective-permute-start(bf16[32,2304]{1,0:T(8,128)(2,1)S(1)} %get-tuple-element.64), channel_id=1, source_target_pairs={{0,24},{8,0},{16,8},{24,16},{1,25},{9,1},{17,9},{25,17},{2,26},{10... | collective-permute-start | bytes 442376 | tf_op jit(solution)/shard_map/ppermute | solution.py:235
  88.4 2.6 %collective-permute-start.21 = (bf16[16,2304]{1,0:T(8,128)(2,1)S(1)}, bf16[16,2304]{1,0:T(8,128)(2,1)S(1)}, u32[]{:S(2)}, u32[]{:S(2)}) collective-permute-start(bf16[16,2304]{1,0:T(8,128)(2,1)S(1)} %get-tuple-element.51), channel_id=1, source_target_pairs={{0,4},{2,6},{4,0},{6,2},{1,5},{3,7},{5,1},{7,3},{8,12},{10,14},{12... | collective-permute-start | bytes 221192 | tf_op jit(solution)/shard_map/ppermute | solution.py:235
  91.0 3.9 %collective-permute-start.22 = (bf16[16,2304]{1,0:T(8,128)(2,1)S(1)}, bf16[16,2304]{1,0:T(8,128)(2,1)S(1)}, u32[]{:S(2)}, u32[]{:S(2)}) collective-permute-start(bf16[16,2304]{1,0:T(8,128)(2,1)S(1)} %get-tuple-element.52), channel_id=1, source_target_pairs={{0,6},{2,0},{4,2},{6,4},{1,7},{3,1},{5,3},{7,5},{8,14},{10,8},{12,... | collective-permute-start | bytes 221192 | tf_op jit(solution)/shard_map/ppermute | solution.py:235
  95.0 2.3 %collective-permute-start.34 = (bf16[16,2304]{1,0:T(8,128)(2,1)S(1)}, bf16[16,2304]{1,0:T(8,128)(2,1)S(1)}, u32[]{:S(2)}, u32[]{:S(2)}) collective-permute-start(bf16[16,2304]{1,0:T(8,128)(2,1)S(1)} %get-tuple-element.67), channel_id=1, source_target_pairs={{0,2},{2,4},{4,6},{6,0},{1,3},{3,5},{5,7},{7,1},{8,10},{10,12},{12... | collective-permute-start | bytes 221192 | tf_op jit(solution)/shard_map/ppermute | solution.py:235
  97.3 2.0 %place.1 = bf16[512,1280]{1,0:T(8,128)(2,1)} custom-call(s32[4]{0:T(128)S(1)} %pad_add_fusion.where_ref, bf16[64,1280]{1,0:T(8,128)(2,1)S(1)} %activate.2.refs_0_, bf16[64,1280]{1,0:T(8,128)(2,1)S(1)} %collective-permute-done.14.refs_1_, bf16[64,1280]{1,0:T(8,128)(2,1)S(1)} %collective-permute-done.15.refs_2_, ...), custom_call_target="tpu_custom_call" | custom-call | bytes 2621440 | tf_op jit(solution)/shard_map/place/pallas_call | solution.py:218
  100.5 2.2 %collective-permute-done.34.refs_3_ = bf16[16,2304]{1,0:T(8,128)(2,1)S(1)} collective-permute-done((bf16[16,2304]{1,0:T(8,128)(2,1)S(1)}, bf16[16,2304]{1,0:T(8,128)(2,1)S(1)}, u32[]{:S(2)}, u32[]{:S(2)}) %collective-permute-start.34) | collective-permute-done | bytes 73760 | tf_op jit(solution)/shard_map/ppermute | solution.py:235
  (74 shorter events, 32.7 us)
Async XLA Ops:
  0.6 14.5 %collective-permute-start.2 = (bf16[16,2304]{1,0:T(8,128)(2,1)}, bf16[16,2304]{1,0:T(8,128)(2,1)S(1)}, u32[]{:S(2)}, u32[]{:S(2)}) collective-permute-start(bf16[16,2304]{1,0:T(8,128)(2,1)} %bitcast.10), channel_id=1, source_target_pairs={{0,6},{2,0},{4,2},{6,4},{1,7},{3,1},{5,3},{7,5},{8,14},{10,8},{12,... | collective-permute-start | bytes 221192 | tf_op jit(solution)/shard_map/ppermute | solution.py:235
  7.0 9.4 %collective-permute-start.1 = (bf16[16,2304]{1,0:T(8,128)(2,1)}, bf16[16,2304]{1,0:T(8,128)(2,1)S(1)}, u32[]{:S(2)}, u32[]{:S(2)}) collective-permute-start(bf16[16,2304]{1,0:T(8,128)(2,1)} %bitcast.11), channel_id=1, source_target_pairs={{0,2},{2,4},{4,6},{6,0},{1,3},{3,5},{5,7},{7,1},{8,10},{10,12},{12... | collective-permute-start | bytes 221192 | tf_op jit(solution)/shard_map/ppermute | solution.py:235
  7.0 9.4 %collective-permute-start = (bf16[16,2304]{1,0:T(8,128)(2,1)}, bf16[16,2304]{1,0:T(8,128)(2,1)S(1)}, u32[]{:S(2)}, u32[]{:S(2)}) collective-permute-start(bf16[16,2304]{1,0:T(8,128)(2,1)} %bitcast.12), channel_id=1, source_target_pairs={{0,4},{2,6},{4,0},{6,2},{1,5},{3,7},{5,1},{7,3},{8,12},{10,14},{12... | collective-permute-start | bytes 221192 | tf_op jit(solution)/shard_map/ppermute | solution.py:235
  16.5 11.6 %collective-permute-start.5 = (bf16[64,2304]{1,0:T(8,128)(2,1)S(1)}, bf16[64,2304]{1,0:T(8,128)(2,1)S(1)}, u32[]{:S(2)}, u32[]{:S(2)}) collective-permute-start(bf16[64,2304]{1,0:T(8,128)(2,1)S(1)} %join.1.refs_0_), channel_id=1, source_target_pairs={{0,16},{8,24},{16,0},{24,8},{1,17},{9,25},{17,1},{25,9},{2,18},{10... | collective-permute-start | bytes 884744 | tf_op jit(solution)/shard_map/ppermute | solution.py:235
  19.6 12.9 %collective-permute-start.4 = (bf16[64,2304]{1,0:T(8,128)(2,1)S(1)}, bf16[64,2304]{1,0:T(8,128)(2,1)S(1)}, u32[]{:S(2)}, u32[]{:S(2)}) collective-permute-start(bf16[64,2304]{1,0:T(8,128)(2,1)S(1)} %join.1.refs_0_), channel_id=1, source_target_pairs={{0,8},{8,16},{16,24},{24,0},{1,9},{9,17},{17,25},{25,1},{2,10},{10... | collective-permute-start | bytes 884744 | tf_op jit(solution)/shard_map/ppermute | solution.py:235
  20.2 12.5 %collective-permute-start.3 = (bf16[64,2304]{1,0:T(8,128)(2,1)S(1)}, bf16[64,2304]{1,0:T(8,128)(2,1)S(1)}, u32[]{:S(2)}, u32[]{:S(2)}) collective-permute-start(bf16[64,2304]{1,0:T(8,128)(2,1)S(1)} %join.1.refs_0_), channel_id=1, source_target_pairs={{0,24},{8,0},{16,8},{24,16},{1,25},{9,1},{17,9},{25,17},{2,26},{10... | collective-permute-start | bytes 884744 | tf_op jit(solution)/shard_map/ppermute | solution.py:235
  22.8 10.4 %collective-permute-start.6 = (bf16[64,2304]{1,0:T(8,128)(2,1)S(1)}, bf16[64,2304]{1,0:T(8,128)(2,1)S(1)}, u32[]{:S(2)}, u32[]{:S(2)}) collective-permute-start(bf16[64,2304]{1,0:T(8,128)(2,1)S(1)} %join.1.refs_0_), channel_id=1, source_target_pairs={{0,1},{1,0},{2,3},{3,2},{4,5},{5,4},{6,7},{7,6},{8,9},{9,8},{10,11... | collective-permute-start | bytes 884744 | tf_op jit(solution)/shard_map/ppermute | solution.py:235
  37.4 8.8 %collective-permute-start.10 = (bf16[64,1280]{1,0:T(8,128)(2,1)S(1)}, bf16[64,1280]{1,0:T(8,128)(2,1)S(1)}, u32[]{:S(2)}, u32[]{:S(2)}) collective-permute-start(bf16[64,1280]{1,0:T(8,128)(2,1)S(1)} %get-tuple-element.42), channel_id=1, source_target_pairs={{0,64},{64,128},{128,192},{192,0},{1,65},{65,129},{129,193},{193,1... | collective-permute-start | bytes 491528 | tf_op jit(solution)/shard_map/ppermute | solution.py:235
  39.1 8.5 %collective-permute-start.11 = (bf16[64,1280]{1,0:T(8,128)(2,1)S(1)}, bf16[64,1280]{1,0:T(8,128)(2,1)S(1)}, u32[]{:S(2)}, u32[]{:S(2)}) collective-permute-start(bf16[64,1280]{1,0:T(8,128)(2,1)S(1)} %get-tuple-element.43), channel_id=1, source_target_pairs={{0,192},{64,0},{128,64},{192,128},{1,193},{65,1},{129,65},{193,129... | collective-permute-start | bytes 491528 | tf_op jit(solution)/shard_map/ppermute | solution.py:235
  39.5 10.9 %collective-permute-start.12 = (bf16[64,1280]{1,0:T(8,128)(2,1)S(1)}, bf16[64,1280]{1,0:T(8,128)(2,1)S(1)}, u32[]{:S(2)}, u32[]{:S(2)}) collective-permute-start(bf16[64,1280]{1,0:T(8,128)(2,1)S(1)} %get-tuple-element.44), channel_id=1, source_target_pairs={{0,128},{64,192},{128,0},{192,64},{1,129},{65,193},{129,1},{193,65... | collective-permute-start | bytes 491528 | tf_op jit(solution)/shard_map/ppermute | solution.py:235
  45.0 8.7 %collective-permute-start.24 = (bf16[64,1280]{1,0:T(8,128)(2,1)S(1)}, bf16[64,1280]{1,0:T(8,128)(2,1)S(1)}, u32[]{:S(2)}, u32[]{:S(2)}) collective-permute-start(bf16[64,1280]{1,0:T(8,128)(2,1)S(1)} %get-tuple-element.56), channel_id=1, source_target_pairs={{0,192},{64,0},{128,64},{192,128},{1,193},{65,1},{129,65},{193,129... | collective-permute-start | bytes 491528 | tf_op jit(solution)/shard_map/ppermute | solution.py:235
  46.2 10.1 %collective-permute-start.25 = (bf16[64,1280]{1,0:T(8,128)(2,1)S(1)}, bf16[64,1280]{1,0:T(8,128)(2,1)S(1)}, u32[]{:S(2)}, u32[]{:S(2)}) collective-permute-start(bf16[64,1280]{1,0:T(8,128)(2,1)S(1)} %get-tuple-element.57), channel_id=1, source_target_pairs={{0,128},{64,192},{128,0},{192,64},{1,129},{65,193},{129,1},{193,65... | collective-permute-start | bytes 491528 | tf_op jit(solution)/shard_map/ppermute | solution.py:235
  56.6 8.8 %collective-permute-start.16 = (bf16[64,1280]{1,0:T(8,128)(2,1)S(1)}, bf16[64,1280]{1,0:T(8,128)(2,1)S(1)}, u32[]{:S(2)}, u32[]{:S(2)}) collective-permute-start(bf16[64,1280]{1,0:T(8,128)(2,1)S(1)} %activate.2.refs_0_), channel_id=1, source_target_pairs={{0,128},{64,192},{128,0},{192,64},{1,129},{65,193},{129,1},{193,65... | collective-permute-start | bytes 491528 | tf_op jit(solution)/shard_map/ppermute | solution.py:235
  58.4 8.5 %collective-permute-start.15 = (bf16[64,1280]{1,0:T(8,128)(2,1)S(1)}, bf16[64,1280]{1,0:T(8,128)(2,1)S(1)}, u32[]{:S(2)}, u32[]{:S(2)}) collective-permute-start(bf16[64,1280]{1,0:T(8,128)(2,1)S(1)} %activate.2.refs_0_), channel_id=1, source_target_pairs={{0,64},{64,128},{128,192},{192,0},{1,65},{65,129},{129,193},{193,1... | collective-permute-start | bytes 491528 | tf_op jit(solution)/shard_map/ppermute | solution.py:235
  59.0 10.7 %collective-permute-start.14 = (bf16[64,1280]{1,0:T(8,128)(2,1)S(1)}, bf16[64,1280]{1,0:T(8,128)(2,1)S(1)}, u32[]{:S(2)}, u32[]{:S(2)}) collective-permute-start(bf16[64,1280]{1,0:T(8,128)(2,1)S(1)} %activate.2.refs_0_), channel_id=1, source_target_pairs={{0,192},{64,0},{128,64},{192,128},{1,193},{65,1},{129,65},{193,129... | collective-permute-start | bytes 491528 | tf_op jit(solution)/shard_map/ppermute | solution.py:235
  61.9 10.3 %collective-permute-start.29 = (bf16[64,1280]{1,0:T(8,128)(2,1)S(1)}, bf16[64,1280]{1,0:T(8,128)(2,1)S(1)}, u32[]{:S(2)}, u32[]{:S(2)}) collective-permute-start(bf16[64,1280]{1,0:T(8,128)(2,1)S(1)} %activate.3.refs_0_.refs_4_), channel_id=1, source_target_pairs={{0,128},{64,192},{128,0},{192,64},{1,129},{65,193},{129,1},{193,65... | collective-permute-start | bytes 491528 | tf_op jit(solution)/shard_map/ppermute | solution.py:235
  63.7 8.5 %collective-permute-start.28 = (bf16[64,1280]{1,0:T(8,128)(2,1)S(1)}, bf16[64,1280]{1,0:T(8,128)(2,1)S(1)}, u32[]{:S(2)}, u32[]{:S(2)}) collective-permute-start(bf16[64,1280]{1,0:T(8,128)(2,1)S(1)} %activate.3.refs_0_.refs_4_), channel_id=1, source_target_pairs={{0,64},{64,128},{128,192},{192,0},{1,65},{65,129},{129,193},{193,1... | collective-permute-start | bytes 491528 | tf_op jit(solution)/shard_map/ppermute | solution.py:235
  65.4 8.4 %collective-permute-start.27 = (bf16[64,1280]{1,0:T(8,128)(2,1)S(1)}, bf16[64,1280]{1,0:T(8,128)(2,1)S(1)}, u32[]{:S(2)}, u32[]{:S(2)}) collective-permute-start(bf16[64,1280]{1,0:T(8,128)(2,1)S(1)} %activate.3.refs_0_.refs_4_), channel_id=1, source_target_pairs={{0,192},{64,0},{128,64},{192,128},{1,193},{65,1},{129,65},{193,129... | collective-permute-start | bytes 491528 | tf_op jit(solution)/shard_map/ppermute | solution.py:235
  77.9 9.5 %collective-permute-start.19 = (bf16[32,2304]{1,0:T(8,128)(2,1)S(1)}, bf16[32,2304]{1,0:T(8,128)(2,1)S(1)}, u32[]{:S(2)}, u32[]{:S(2)}) collective-permute-start(bf16[32,2304]{1,0:T(8,128)(2,1)S(1)} %get-tuple-element.49), channel_id=1, source_target_pairs={{0,24},{8,0},{16,8},{24,16},{1,25},{9,1},{17,9},{25,17},{2,26},{10... | collective-permute-start | bytes 442376 | tf_op jit(solution)/shard_map/ppermute | solution.py:235
  79.7 8.6 %collective-permute-start.20 = (bf16[32,2304]{1,0:T(8,128)(2,1)S(1)}, bf16[32,2304]{1,0:T(8,128)(2,1)S(1)}, u32[]{:S(2)}, u32[]{:S(2)}) collective-permute-start(bf16[32,2304]{1,0:T(8,128)(2,1)S(1)} %get-tuple-element.50), channel_id=1, source_target_pairs={{0,16},{8,24},{16,0},{24,8},{1,17},{9,25},{17,1},{25,9},{2,18},{10... | collective-permute-start | bytes 442376 | tf_op jit(solution)/shard_map/ppermute | solution.py:235
  84.0 10.9 %collective-permute-start.31 = (bf16[32,2304]{1,0:T(8,128)(2,1)S(1)}, bf16[32,2304]{1,0:T(8,128)(2,1)S(1)}, u32[]{:S(2)}, u32[]{:S(2)}) collective-permute-start(bf16[32,2304]{1,0:T(8,128)(2,1)S(1)} %get-tuple-element.63), channel_id=1, source_target_pairs={{0,8},{8,16},{16,24},{24,0},{1,9},{9,17},{17,25},{25,1},{2,10},{10... | collective-permute-start | bytes 442376 | tf_op jit(solution)/shard_map/ppermute | solution.py:235
  84.8 10.2 %collective-permute-start.32 = (bf16[32,2304]{1,0:T(8,128)(2,1)S(1)}, bf16[32,2304]{1,0:T(8,128)(2,1)S(1)}, u32[]{:S(2)}, u32[]{:S(2)}) collective-permute-start(bf16[32,2304]{1,0:T(8,128)(2,1)S(1)} %get-tuple-element.64), channel_id=1, source_target_pairs={{0,24},{8,0},{16,8},{24,16},{1,25},{9,1},{17,9},{25,17},{2,26},{10... | collective-permute-start | bytes 442376 | tf_op jit(solution)/shard_map/ppermute | solution.py:235
  88.4 11.0 %collective-permute-start.21 = (bf16[16,2304]{1,0:T(8,128)(2,1)S(1)}, bf16[16,2304]{1,0:T(8,128)(2,1)S(1)}, u32[]{:S(2)}, u32[]{:S(2)}) collective-permute-start(bf16[16,2304]{1,0:T(8,128)(2,1)S(1)} %get-tuple-element.51), channel_id=1, source_target_pairs={{0,4},{2,6},{4,0},{6,2},{1,5},{3,7},{5,1},{7,3},{8,12},{10,14},{12... | collective-permute-start | bytes 221192 | tf_op jit(solution)/shard_map/ppermute | solution.py:235
  91.0 9.5 %collective-permute-start.22 = (bf16[16,2304]{1,0:T(8,128)(2,1)S(1)}, bf16[16,2304]{1,0:T(8,128)(2,1)S(1)}, u32[]{:S(2)}, u32[]{:S(2)}) collective-permute-start(bf16[16,2304]{1,0:T(8,128)(2,1)S(1)} %get-tuple-element.52), channel_id=1, source_target_pairs={{0,6},{2,0},{4,2},{6,4},{1,7},{3,1},{5,3},{7,5},{8,14},{10,8},{12,... | collective-permute-start | bytes 221192 | tf_op jit(solution)/shard_map/ppermute | solution.py:235
  (16 other events, 122.5 us)
